TPU v7x, 512 devices: a whole 4x8x8 slice. The times are simulated.
512 devices in a mesh: slab: 8 (over x, core), brick: 64 (over y, z).
Axes of the slice: x: 4, y: 8, z: 8, core: 2. Of those that a mesh axis runs over, the one named last changes fastest.
Arguments:
- position: float32 [3, 131072], P(None, ('slab', 'brick')), may hold values from 0 to 1
- orient: float32 [4, 131072], P(None, ('slab', 'brick')), may hold values from -0.5 to 1, as said below
- velocity: float32 [6, 131072], P(None, ('slab', 'brick')), may hold values from -3 to 3
- history: float32 [64, 131072], P(None, ('slab', 'brick')), may hold values from 0 to 1
- template: float32 [3, 64], replicated, may hold values from -1.4 to 1.4
- cross_local: int32 [32768], P(('slab', 'brick')), may hold values from 0 to 255
- cross_ghost: int32 [32768], P(('slab', 'brick')), may hold values from 0 to 511
- cross_count: int32 [512], P(('slab', 'brick')), may hold values from 8 to 64, as said below
- inner_first: int32 [32768], P(('slab', 'brick')), may hold values from 0 to 255
- inner_gap: int32 [32768], P(('slab', 'brick')), may hold values from 1 to 255
- mig_index: int32 [32768], P(('slab', 'brick')), may hold values from 0 to 255, as said below
- mig_dest: int32 [32768, 1], P(('slab', 'brick')), may hold values from 0 to 63; in each aligned block of 64 rows (0 to 63, 64 to 127, ...) at most 2 rows name the same one
Outputs:
- staying: float32 [77, 131072], P(None, ('slab', 'brick'))
- arrivals: float32 [77, 65536], P(None, ('slab', 'brick'))
Inputs may be any that keep to these rules, and one draw needn't show every extreme that they name: `orient`: the scalar part lies in 0.6 to 1.0, the other three in -0.5 to 0.5. `cross_count`: at least 8; some brick has exactly 64 in every draw. `mig_index`: 64 distinct clumps of each brick. `mig_dest`: among the 64 migrants of one brick at most 2 go to one destination, and exactly 2 do in some bricks.
All inputs are finite; a program needn't handle non-finite values.
Results may differ from a plain program's by a relative error of at most 0.0003.
Values sent between devices are 32-bit elements; how exact they have to be, the bound alone decides.
No kernel may reach another device: no remote copies, remote signals or barrier semaphores. Data moves between devices by JAX's collectives and lax.ppermute only.
A program may use at most 64 MiB of HBM per device.

v0:
```python
import math

import jax
import jax.numpy as jnp
from jax import lax
from jax.sharding import PartitionSpec as P

SLOT_CAP = 2


diameter = 0.3
stiffness = 20.0
softening = 0.0001
time_step = 0.02
inertia_scale = 0.05
history_decay = 0.9


def from_behind(value, axis, steps):
    count = lax.axis_size(axis)
    pairs = [(source, (source + steps) % count) for source in range(count)]
    return lax.ppermute(value, axis, pairs)


def rotation(orient):
    length = jnp.sqrt(jnp.sum(orient * orient, axis=0))
    unit_quat = orient / length
    qw = unit_quat[0]
    qx = unit_quat[1]
    qy = unit_quat[2]
    qz = unit_quat[3]
    matrix_rows = [
        [1.0 - 2.0 * (qy * qy + qz * qz), 2.0 * (qx * qy - qw * qz), 2.0 * (qx * qz + qw * qy)],
        [2.0 * (qx * qy + qw * qz), 1.0 - 2.0 * (qx * qx + qz * qz), 2.0 * (qy * qz - qw * qx)],
        [2.0 * (qx * qz - qw * qy), 2.0 * (qy * qz + qw * qx), 1.0 - 2.0 * (qx * qx + qy * qy)],
    ]
    return jnp.stack([jnp.stack(entry) for entry in matrix_rows])


def arms(orient, template):
    return jnp.einsum("ijc,jm->imc", rotation(orient), template, precision=lax.Precision.HIGHEST)


def contact_block(arm_a, pos_a, hist_a, arm_b, pos_b, hist_b, active):
    place_a = pos_a[:, None, :] + arm_a
    place_b = pos_b[:, None, :] + arm_b
    offset = place_a[:, :, None, :] - place_b[:, None, :, :]
    distance = jnp.sqrt(jnp.sum(offset * offset, axis=0) + softening)
    margin = jnp.maximum(diameter - distance, 0.0) * active
    magnitude = (
        stiffness * margin * (1.0 + 0.5 * (hist_a[:, None, :] + hist_b[None, :, :])) / distance
    )
    pair_push = magnitude[None] * offset
    force_a = jnp.sum(pair_push, axis=2)
    force_b = -jnp.sum(pair_push, axis=1)
    row_a = jnp.concatenate(
        [jnp.sum(force_a, 1), jnp.sum(jnp.cross(arm_a, force_a, axis=0), 1), jnp.sum(margin, 1)], 0
    )
    row_b = jnp.concatenate(
        [jnp.sum(force_b, 1), jnp.sum(jnp.cross(arm_b, force_b, axis=0), 1), jnp.sum(margin, 0)], 0
    )
    return (row_a, row_b)


def pair_terms(source_a, source_b, index_a, index_b, active, count_a, count_b):
    arm_a_all, pos_a_all, hist_a_all = source_a
    arm_b_all, pos_b_all, hist_b_all = source_b
    pair_total = index_a.shape[0]
    block_size = math.gcd(64, pair_total)
    blocks = pair_total // block_size

    def accumulate(totals_now, block_data):
        sel_a, sel_b, sel_active = block_data
        row_a, row_b = contact_block(
            arm_a_all[:, :, sel_a],
            pos_a_all[:, sel_a],
            hist_a_all[:, sel_a],
            arm_b_all[:, :, sel_b],
            pos_b_all[:, sel_b],
            hist_b_all[:, sel_b],
            sel_active,
        )
        return (
            (totals_now[0].at[:, sel_a].add(row_a), totals_now[1].at[:, sel_b].add(row_b)),
            None,
        )

    starting = (jnp.zeros((70, count_a), jnp.float32), jnp.zeros((70, count_b), jnp.float32))
    totals, unused = lax.scan(
        accumulate,
        starting,
        (
            index_a.reshape(blocks, block_size),
            index_b.reshape(blocks, block_size),
            active.reshape(blocks, block_size),
        ),
    )
    return totals


def advance(position, orient, velocity, history, totals):
    net_force = totals[0:3]
    torque = totals[3:6]
    margin_sum = totals[6:]
    linear = velocity[0:3] + time_step * net_force
    angular = velocity[3:6] + time_step * torque / inertia_scale
    moved_pos = position + time_step * linear
    spin_scalar = -jnp.sum(angular * orient[1:4], 0, keepdims=True)
    spin_vector = orient[0:1] * angular + jnp.cross(angular, orient[1:4], axis=0)
    turned = orient + 0.5 * time_step * jnp.concatenate([spin_scalar, spin_vector], 0)
    recalled = history_decay * history + margin_sum
    return jnp.concatenate([moved_pos, turned, linear, angular, recalled], 0)


def depart(new_state, leaving, target, slots_each, bricks):
    moving = leaving.shape[0]
    earlier = jnp.arange(moving)[:, None] > jnp.arange(moving)[None, :]
    same_target = target[:, None] == target[None, :]
    slot_rank = jnp.sum((earlier & same_target).astype(jnp.int32), 1)
    column = target * slots_each + slot_rank
    buffer = (
        jnp.zeros((new_state.shape[0], bricks * slots_each), jnp.float32)
        .at[:, column]
        .set(new_state[:, leaving])
    )
    departed = jnp.any(
        leaving[:, None] == jnp.arange(new_state.shape[1]).astype(jnp.int32)[None, :], 0
    )
    remaining = jnp.where(departed[None, :], 0.0, new_state)
    return (remaining, buffer)


def shards(
    position,
    orient,
    velocity,
    history,
    template,
    cross_local,
    cross_ghost,
    cross_count,
    inner_first,
    inner_gap,
    mig_index,
    mig_dest,
):
    clumps = position.shape[1]
    members = template.shape[1]
    slot_total = cross_local.shape[0]
    arm_here = arms(orient, template)
    brick_shift = jnp.array([[0.0], [1.0], [0.0]], jnp.float32)
    slab_shift = jnp.array([[1.0], [0.0], [0.0]], jnp.float32)
    near_side = cross_ghost < clumps
    slot_offset = jnp.where(near_side[None, :], brick_shift, slab_shift)
    packed = jnp.concatenate([arm_here.reshape(3 * members, clumps), position, history], 0)
    from_brick = from_behind(packed, "brick", -1)
    from_slab = from_behind(packed, "slab", -1)
    picked = jnp.concatenate([from_brick, from_slab], 1)[:, cross_ghost]
    far_arm = picked[0 : 3 * members].reshape(3, members, slot_total)
    far_pos = picked[3 * members : 3 * members + 3] + slot_offset
    far_hist = picked[3 * members + 3 :]
    local_set = (arm_here, position, history)
    second = (inner_first + inner_gap) % clumps
    inner_a, inner_b = pair_terms(
        local_set,
        local_set,
        inner_first,
        second,
        jnp.ones(inner_first.shape, jnp.float32),
        clumps,
        clumps,
    )
    active = (jnp.arange(slot_total) < cross_count[0]).astype(jnp.float32)
    slot_numbers = jnp.arange(slot_total, dtype=jnp.int32)
    cross_a, far_back = pair_terms(
        local_set,
        (far_arm, far_pos, far_hist),
        cross_local,
        slot_numbers,
        active,
        clumps,
        slot_total,
    )
    columns = jnp.zeros((70, 2 * clumps), jnp.float32).at[:, cross_ghost].add(far_back)
    back_brick = from_behind(columns[:, :clumps], "brick", 1)
    back_slab = from_behind(columns[:, clumps:], "slab", 1)
    totals = inner_a + inner_b + cross_a + back_brick + back_slab
    new_state = advance(position, orient, velocity, history, totals)
    remaining, buffer = depart(
        new_state, mig_index, mig_dest[:, 0], SLOT_CAP, lax.axis_size("brick")
    )
    arrivals = lax.all_to_all(buffer, "brick", split_axis=1, concat_axis=1, tiled=True)
    return (remaining, arrivals)


def solution(mesh):
    return jax.shard_map(
        shards,
        mesh=mesh,
        in_specs=(
            P(None, ("slab", "brick")),
            P(None, ("slab", "brick")),
            P(None, ("slab", "brick")),
            P(None, ("slab", "brick")),
            P(),
            P(("slab", "brick")),
            P(("slab", "brick")),
            P(("slab", "brick")),
            P(("slab", "brick")),
            P(("slab", "brick")),
            P(("slab", "brick")),
            P(("slab", "brick"), None),
        ),
        out_specs=(P(None, ("slab", "brick")), P(None, ("slab", "brick"))),
        check_vma=False,
    )
```

profile of v0, /device:TPU:6, one launch (start us, length us, event | category | flops | bytes accessed | tf_op | source)
XLA Modules:
  0.0 77.4 jit_solution(15299666284865571626)
XLA Ops:
  0.7 0.7 multiply_reduce_fusion.1
  1.4 0.7 broadcast_divide_fusion
  2.1 0.9 %copy.336 = f32[64,256]{0,1:T(8,128)S(1)} copy(f32[64,256]{1,0:T(8,128)} %param.19) | data formatting | bytes 131072 | tf_op args[3]
  3.1 0.8 %copy.330 = f32[3,256]{0,1:T(8,128)S(1)} copy(f32[3,256]{1,0:T(4,128)} %param.16) | data formatting | bytes 6144 | tf_op args[0]
  3.9 0.4 fusion.22
  4.3 0.1 copy.334
  4.5 0.2 pad_maximum_fusion.1
  4.7 0.3 collective-permute-start.1
  4.9 13.8 %collective-permute-start = (f32[259,256]{0,1:T(8,128)S(1)}, f32[259,256]{0,1:T(8,128)S(1)}, u32[]{:S(2)}, u32[]{:S(2)}) collective-permute-start(f32[259,256]{0,1:T(8,128)S(1)} %pad_maximum_fusion.1), channel_id=1, source_target_pairs={{0,63},{1,0},{2,1},{3,2},{4,3},{5,4},{6,5},{7,6},{8,7},{9,8},{10,9... | collective-permute-start | bytes 795656 | tf_op jit(solution)/shard_map/ppermute | solution.py:22
  18.8 0.7 compare_select_fusion.5
  19.5 0.7 broadcast_compare_fusion
  20.1 0.7 compare_select_fusion
  20.8 0.7 fusion.14
  21.5 0.7 compare_select_fusion.3
  22.2 0.6 gather_fusion.12
  22.8 0.6 gather_fusion.9
  23.4 0.6 gather_fusion.11
  24.0 0.6 gather_fusion.7
  24.6 0.2 copy.332
  24.8 0.7 gather_fusion.10
  25.5 0.7 gather_fusion.8
  26.8 0.2 convert_reduce_fusion
  27.4 0.1 copy.353
  27.5 0.1 copy.349
  27.7 1.1 %fusion.7 = f32[64,64,64]{2,1,0:T(8,128)S(1)} fusion(f32[3,64,64]{2,1,0:T(8,128)S(1)} %bitcast_add_fusion, f32[3,64,64]{2,1,0:T(8,128)S(1)} %bitcast_add_fusion.1), kind=kLoop, calls=%fused_computation.29 | loop fusion | flops 2097152 | bytes 1146880 | tf_op jit(solution)/shard_map/while/body/eval_jaxpr/reduce_sum | solution.py:48
  28.8 1.7 %fusion.9 = (f32[64,64]{1,0:T(8,128)S(1)}, f32[64,64]{1,0:T(8,128)S(1)}, f32[64,64,64]{2,1,0:T(8,128)S(1)}) fusion(f32[64,64,64]{2,1,0:T(8,128)S(1)} %fusion.7, f32[64,64]{1,0:T(8,128)S(1)} %copy.357, f32[64,64]{1,0:T(8,128)S(1)} %copy.355), kind=kLoop, calls=%fused_computation.33 | loop fusion | flops 2875392 | bytes 2162688 | tf_op jit(solution)/shard_map/while/body/eval_jaxpr/reduce_sum | solution.py:57
  30.4 1.6 %fusion.1 = (f32[3,64,64]{2,1,0:T(8,128)S(1)}, f32[3,64,64]{2,1,0:T(8,128)S(1)}, f32[3,64]{1,0:T(4,128)S(1)}) fusion(f32[64,64,64]{2,1,0:T(8,128)S(1)} %get-tuple-element.92, f32[3,64,64]{2,1,0:T(8,128)S(1)} %bitcast_add_fusion, f32[3,64,64]{2,1,0:T(8,128)S(1)} %bitcast_add_fusion.1), kind=kLoop, calls=%fused_computation.21 | loop fusion | flops 3907392 | bytes 1245952 | tf_op jit(solution)/shard_map/while/body/eval_jaxpr/reduce_sum | solution.py:54
  32.2 0.6 gather_fusion.5
  32.8 0.6 gather_fusion
  33.4 0.7 gather_fusion.1
  34.2 0.1 copy.333
  34.5 0.7 gather_fusion.2
  35.4 0.6 gather_fusion.3
  36.1 0.6 gather_fusion.6
  36.7 0.1 copy.338
  36.8 0.1 copy.339
  37.0 0.7 gather_fusion.4
  37.6 0.1 copy.340
  37.8 1.1 %fusion.6 = f32[64,64,64]{2,1,0:T(8,128)S(1)} fusion(f32[3,64,64]{2,1,0:T(8,128)S(1)} %bitcast_add_fusion.2, f32[3,64,64]{2,1,0:T(8,128)S(1)} %bitcast_add_fusion.3), kind=kLoop, calls=%fused_computation.28 | loop fusion | flops 2097152 | bytes 1146880 | tf_op jit(solution)/shard_map/while/body/eval_jaxpr/reduce_sum | solution.py:48
  38.8 1.7 %fusion.10 = (f32[64,64]{1,0:T(8,128)S(1)}, f32[64,64]{1,0:T(8,128)S(1)}, f32[64,64,64]{2,1,0:T(8,128)S(1)}) fusion(f32[64,64,64]{2,1,0:T(8,128)S(1)} %fusion.6, f32[64]{0:T(128)S(1)} %compare_convert_fusion, f32[64,64]{1,0:T(8,128)S(1)} %copy.343, f32[64,64]{1,0:T(8,128)S(1)} %copy.342), kind=kLoop, calls=%fused_computation.37 | loop fusion | flops 3137536 | bytes 2162944 | tf_op jit(solution)/shard_map/while/body/eval_jaxpr/reduce_sum | solution.py:57
  40.6 1.6 %fusion.3 = (f32[3,64,64]{2,1,0:T(8,128)S(1)}, f32[3,64,64]{2,1,0:T(8,128)S(1)}, f32[3,64]{1,0:T(4,128)S(1)}) fusion(f32[64,64,64]{2,1,0:T(8,128)S(1)} %get-tuple-element.91, f32[3,64,64]{2,1,0:T(8,128)S(1)} %bitcast_add_fusion.2, f32[3,64,64]{2,1,0:T(8,128)S(1)} %bitcast_add_fusion.3), kind=kLoop, calls=%fused_computation.25 | loop fusion | flops 3907392 | bytes 1245952 | tf_op jit(solution)/shard_map/while/body/eval_jaxpr/reduce_sum | solution.py:54
  42.3 0.1 copy.345
  42.4 0.8 %scatter_custom_fusion = f32[70,64]{0,1:T(8,128)S(1)} fusion(s32[64]{0:T(128)S(1)} %iota.31, f32[64,70]{1,0:T(8,128)S(1)} %copy.345, f32[]{:T(128)} %constant.56.clone.1), kind=kCustom, calls=%fused_computation.80 | custom fusion | flops 4480 | bytes 17924 | tf_op jit(solution)/shard_map/while/body/eval_jaxpr/scatter-add | solution.py:84
  43.2 0.9 %scatter_custom_fusion.1 = f32[70,512]{0,1:T(8,128)S(1)} fusion(s32[64]{0:T(128)S(1)} %compare_select_fusion.5, f32[]{:T(128)} %constant.56.clone.1, f32[70,64]{0,1:T(8,128)S(1)} %scatter_custom_fusion), kind=kCustom, calls=%fused_computation.43 | custom fusion | flops 4480 | bytes 176132 | tf_op jit(solution)/shard_map/scatter-add | solution.py:184
  44.2 1.9 %collective-permute-start.2 = (f32[70,256]{0,1:T(8,128)S(1)}, f32[70,256]{0,1:T(8,128)S(1)}, u32[]{:S(2)}, u32[]{:S(2)}) collective-permute-start(f32[70,256]{0,1:T(8,128)S(1)} %get-tuple-element.94), channel_id=1, source_target_pairs={{0,1},{1,2},{2,3},{3,4},{4,5},{5,6},{6,7},{7,8},{8,9},{9,10},{10,1... | collective-permute-start | bytes 215048 | tf_op jit(solution)/shard_map/ppermute | solution.py:22
  46.2 0.1 maximum_bitcast_fusion
  46.3 0.1 copy.361
  46.4 2.2 %collective-permute-done.3 = f32[70,256]{0,1:T(8,128)S(1)} collective-permute-done((f32[70,256]{0,1:T(8,128)S(1)}, f32[70,256]{0,1:T(8,128)S(1)}, u32[]{:S(2)}, u32[]{:S(2)}) %collective-permute-start.3) | collective-permute-done | bytes 71712 | tf_op jit(solution)/shard_map/ppermute | solution.py:22
  48.6 5.8 %collective-permute-done.2 = f32[70,256]{0,1:T(8,128)S(1)} collective-permute-done((f32[70,256]{0,1:T(8,128)S(1)}, f32[70,256]{0,1:T(8,128)S(1)}, u32[]{:S(2)}, u32[]{:S(2)}) %collective-permute-start.2) | collective-permute-done | bytes 71712 | tf_op jit(solution)/shard_map/ppermute | solution.py:22
  54.4 1.8 %scatter_fusion = f32[70,256]{0,1:T(8,128)S(1)} fusion(f32[70,256]{0,1:T(8,128)S(1)} %add.286, s32[192]{0:T(256)S(1)} %bitcast.129, f32[192,70]{1,0:T(8,128)S(1)} %copy.361), kind=kCustom, calls=%fused_computation.16 | custom fusion | flops 13440 | bytes 162048 | tf_op jit(solution)/shard_map/add | solution.py:187
  56.3 0.1 slice_add_fusion
  56.4 0.1 fusion.36
  56.6 0.1 copy.375
  56.7 0.1 copy.368
  56.9 0.1 copy.366
  57.0 0.1 copy.365
  57.2 0.1 copy.367
  57.3 0.2 concatenate.55
  57.6 1.5 %scatter_custom_fusion.3 = f32[77,128]{0,1:T(8,128)} fusion(s32[64]{0:T(128)S(1)} %fusion.31, f32[77,256]{0,1:T(8,128)S(1)} %concatenate.55, s32[1024]{0:T(1024)S(1)} %pad_clamp_fusion, f32[]{:T(128)} %constant.56.clone.1), kind=kCustom, calls=%fused_computation.74 | custom fusion | bytes 39428 | tf_op jit(solution)/shard_map/scatter | solution.py:124
  59.1 5.1 %all-to-all-start = ((f32[77,64,2]{0,2,1:T(2,128)}), f32[77,64,2]{0,2,1:T(2,128)S(1)}, u32[]{:S(2)}, u32[]{:S(2)}) async-start(f32[77,64,2]{0,2,1:T(2,128)} %bitcast.62), calls=%async_computation | async-start | bytes 131072 | tf_op jit(solution)/shard_map/all_to_all | solution.py:192
  64.2 0.1 broadcast_select_fusion
  64.3 0.7 copy.369
  65.0 11.7 %all-to-all-done = f32[77,64,2]{0,2,1:T(2,128)S(1)} async-done(((f32[77,64,2]{0,2,1:T(2,128)}), f32[77,64,2]{0,2,1:T(2,128)S(1)}, u32[]{:S(2)}, u32[]{:S(2)}) %all-to-all-start) | async-done | bytes 39456 | tf_op jit(solution)/shard_map/all_to_all | solution.py:192
  76.7 0.7 copy.370
  (74 shorter events, 1.5 us)
Async XLA Ops:
  0.6 3.3 %copy-start = (f32[3,64]{1,0:T(4,128)S(1)}, f32[3,64]{1,0:T(4,128)}, u32[]{:S(2)}) copy-start(f32[3,64]{1,0:T(4,128)} %param.20) | copy-start | bytes 2308
  0.6 26.2 %copy-start.6 = (s32[64,1]{0,1:T(1,128)S(1)}, s32[64,1]{0,1:T(1,128)}, u32[]{:S(2)}) copy-start(s32[64,1]{0,1:T(1,128)} %param.27) | copy-start | bytes 772
  0.7 26.4 %copy-start.7 = (s32[64]{0:T(128)S(1)}, s32[64]{0:T(128)}, u32[]{:S(2)}) copy-start(s32[64]{0:T(128)} %param.21) | copy-start | bytes 772
  4.7 29.8 %collective-permute-start.1 = (f32[259,256]{0,1:T(8,128)S(1)}, f32[259,256]{0,1:T(8,128)S(1)}, u32[]{:S(2)}, u32[]{:S(2)}) collective-permute-start(f32[259,256]{0,1:T(8,128)S(1)} %pad_maximum_fusion.1), channel_id=1, source_target_pairs={{0,448},{64,0},{128,64},{192,128},{256,192},{320,256},{384,320},{4... | collective-permute-start | bytes 795656 | tf_op jit(solution)/shard_map/ppermute | solution.py:22
  4.9 29.5 %collective-permute-start = (f32[259,256]{0,1:T(8,128)S(1)}, f32[259,256]{0,1:T(8,128)S(1)}, u32[]{:S(2)}, u32[]{:S(2)}) collective-permute-start(f32[259,256]{0,1:T(8,128)S(1)} %pad_maximum_fusion.1), channel_id=1, source_target_pairs={{0,63},{1,0},{2,1},{3,2},{4,3},{5,4},{6,5},{7,6},{8,7},{9,8},{10,9... | collective-permute-start | bytes 795656 | tf_op jit(solution)/shard_map/ppermute | solution.py:22
  32.2 3.1 %copy-start.4 = (f32[3]{0:T(128)S(1)}, f32[3]{0:T(128)}, u32[]{:S(2)}) copy-start(f32[3]{0:T(128)} %constant.120) | copy-start | bytes 40
  32.2 3.1 %copy-start.5 = (f32[3]{0:T(128)S(1)}, f32[3]{0:T(128)}, u32[]{:S(2)}) copy-start(f32[3]{0:T(128)} %constant.119) | copy-start | bytes 40
  44.1 12.5 %copy-start.1 = (f32[4,256]{1,0:T(4,128)S(1)}, f32[4,256]{1,0:T(4,128)}, u32[]{:S(2)}) copy-start(f32[4,256]{1,0:T(4,128)} %param.17) | copy-start | bytes 12292
  44.1 12.5 %copy-start.2 = (f32[3,256]{1,0:T(4,128)S(1)}, f32[3,256]{1,0:T(4,128)}, u32[]{:S(2)}) copy-start(f32[3,256]{1,0:T(4,128)} %param.16) | copy-start | bytes 9220
  44.1 12.5 %copy-start.3 = (f32[6,256]{1,0:T(8,128)S(1)}, f32[6,256]{1,0:T(8,128)}, u32[]{:S(2)}) copy-start(f32[6,256]{1,0:T(8,128)} %param.18) | copy-start | bytes 18436
  44.2 12.7 %slice-start = ((f32[4,256]{1,0:T(4,128)}), f32[1,256]{1,0:T(1,128)S(1)}, s32[]{:S(2)}) async-start(f32[4,256]{1,0:T(4,128)} %param.17), calls=%async_computation.1 | async-start | bytes 2048 | tf_op jit(solution)/shard_map/slice | solution.py:109
  44.2 4.4 %collective-permute-start.3 = (f32[70,256]{0,1:T(8,128)S(1)}, f32[70,256]{0,1:T(8,128)S(1)}, u32[]{:S(2)}, u32[]{:S(2)}) collective-permute-start(f32[70,256]{0,1:T(8,128)S(1)} %get-tuple-element.93), channel_id=1, source_target_pairs={{0,64},{64,128},{128,192},{192,256},{256,320},{320,384},{384,448},... | collective-permute-start | bytes 215048 | tf_op jit(solution)/shard_map/ppermute | solution.py:22
  44.2 10.2 %collective-permute-start.2 = (f32[70,256]{0,1:T(8,128)S(1)}, f32[70,256]{0,1:T(8,128)S(1)}, u32[]{:S(2)}, u32[]{:S(2)}) collective-permute-start(f32[70,256]{0,1:T(8,128)S(1)} %get-tuple-element.94), channel_id=1, source_target_pairs={{0,1},{1,2},{2,3},{3,4},{4,5},{5,6},{6,7},{7,8},{8,9},{9,10},{10,1... | collective-permute-start | bytes 215048 | tf_op jit(solution)/shard_map/ppermute | solution.py:22
  59.1 17.6 %all-to-all-start = ((f32[77,64,2]{0,2,1:T(2,128)}), f32[77,64,2]{0,2,1:T(2,128)S(1)}, u32[]{:S(2)}, u32[]{:S(2)}) async-start(f32[77,64,2]{0,2,1:T(2,128)} %bitcast.62), calls=%async_computation | async-start | bytes 131072 | tf_op jit(solution)/shard_map/all_to_all | solution.py:192
where the time goes:
time: 78.6 us; the launch traced here: 77.4 us
  starting transfers between devices  21.1 us (27%)
  waiting for transfers between devices  19.6 us (25%)
  other arithmetic  18.5 us (24%)
  local copies, waits for them, and re-layouts  15.8 us (20%)
  between operations  1.93 us (2%)
    ppermute x4, starting transfers between devices, from_behind(): return lax.ppermute(value, axis, pairs)  16.1 us
    all_to_all x1, waiting for transfers between devices, shards(): lax.all_to_all(buffer, 'brick', split_axis=1, concat_axis=1, tiled=True)  11.7 us
    ppermute x4, waiting for transfers between devices, from_behind(): return lax.ppermute(value, axis, pairs)  8 us
    all_to_all x1, starting transfers between devices, shards(): lax.all_to_all(buffer, 'brick', split_axis=1, concat_axis=1, tiled=True)  5.09 us
    unnamed x22, local copies, waits for them, and re-layouts  3.41 us
    reduce_sum x2, other arithmetic, contact_block(): jnp.sum(margin, 1)  3.39 us
    reduce_sum x2, other arithmetic, contact_block(): force_a = jnp.sum(pair_push, axis=2)  3.27 us
    reduce_sum x2, other arithmetic, contact_block(): distance = jnp.sqrt(jnp.sum(offset * offset, axis=0) + softening)  2.18 us
  transfers between devices with their start and end apart: 5, of which 3 were waited for; matrix products, arithmetic and copies ran while one was open for 21% of the time, Pallas kernels for 0%

commit v1 on v0

v1 whole, which is shorter than its diff:
```python
import jax
import jax.numpy as jnp
from jax import lax
from jax.experimental import pallas as pl
from jax.experimental.pallas import tpu as pltpu
from jax.sharding import PartitionSpec as P

MEMBERS = 64
CLUMPS = 256
LANES = 128
PAIRS = 64
HALF = MEMBERS // 2
SLOT_CAP = 2
IDLE = 1024

DIAMETER = 0.3
SOFTENING = 0.0001
TIME_STEP = 0.02
INERTIA_SCALE = 0.05
HISTORY_DECAY = 0.9

POS = MEMBERS
ORI = MEMBERS + 3
LISTS = MEMBERS + 7
PACKED = MEMBERS + 8

F32 = jnp.float32
BF16 = jnp.bfloat16
I32 = jnp.int32


def parts_of(value):
    high = value.astype(BF16)
    rest = value - high.astype(F32)
    middle = rest.astype(BF16)
    low = (rest - middle.astype(F32)).astype(BF16)
    return (high, middle, low)


def one_hot(index_row, rows=CLUMPS):
    count = lax.broadcasted_iota(I32, (rows, index_row.shape[1]), 0)
    return jnp.where(count == index_row, 1.0, 0.0).astype(F32).astype(BF16)


def gather(parts, chosen):
    high, middle, low = [jnp.dot(part, chosen, preferred_element_type=F32) for part in parts]
    return high + middle + low


def scatter(value, chosen):
    dims = (((1,), (1,)), ((), ()))
    high, middle, low = [
        lax.dot_general(part, chosen, dims, preferred_element_type=F32) for part in parts_of(value)
    ]
    return high + middle + low


def arms_of(picked, template):
    quat = [picked[ORI + k : ORI + k + 1] for k in range(4)]
    scale = lax.rsqrt(quat[0] * quat[0] + quat[1] * quat[1] + quat[2] * quat[2] + quat[3] * quat[3])
    qw, qx, qy, qz = [q * scale for q in quat]
    matrix = [
        [1.0 - 2.0 * (qy * qy + qz * qz), 2.0 * (qx * qy - qw * qz), 2.0 * (qx * qz + qw * qy)],
        [2.0 * (qx * qy + qw * qz), 1.0 - 2.0 * (qx * qx + qz * qz), 2.0 * (qy * qz - qw * qx)],
        [2.0 * (qx * qz - qw * qy), 2.0 * (qy * qz + qw * qx), 1.0 - 2.0 * (qx * qx + qy * qy)],
    ]
    return [row[0] * template[0] + row[1] * template[1] + row[2] * template[2] for row in matrix]


def spread_template(template_ref):
    padded = jnp.concatenate([template_ref[...], jnp.zeros((5, MEMBERS), F32)], 0)
    turned = padded.T
    return [jnp.broadcast_to(turned[:, k : k + 1], (MEMBERS, LANES)) for k in range(3)]


def halves(value):
    lane = lax.broadcasted_iota(I32, (HALF, LANES), 1)
    return jnp.where(lane < PAIRS, value[:HALF], value[HALF:])


def place_source(src_ref, picked, arm, shift):
    for k in range(3):
        src_ref[k] = (picked[POS + k : POS + k + 1] + shift[k]) + arm[k]
    src_ref[3] = 10.0 + 10.0 * picked[0:MEMBERS]


def contact(place, weight, src_ref):
    def step(b, sums):
        other = [src_ref[k, pl.ds(b, 1), :] for k in range(4)]
        dx = place[0] - other[0]
        dy = place[1] - other[1]
        dz = place[2] - other[2]
        square = dx * dx + dy * dy + (dz * dz + SOFTENING)
        inverse = lax.rsqrt(square)
        margin = jnp.maximum(DIAMETER - square * inverse, 0.0)
        push = margin * inverse * (weight + other[3])
        return (sums[0] + push * dx, sums[1] + push * dy, sums[2] + push * dz, sums[3] + margin)

    zero = jnp.zeros((HALF, LANES), F32)
    return lax.fori_loop(0, MEMBERS, step, (zero, zero, zero, zero), unroll=4)


def body_rows(arm, force):
    turn = [
        arm[1] * force[2] - arm[2] * force[1],
        arm[2] * force[0] - arm[0] * force[2],
        arm[0] * force[1] - arm[1] * force[0],
    ]
    return jnp.concatenate(
        [jnp.sum(v, axis=0, keepdims=True) for v in list(force) + turn]
        + [jnp.zeros((2, LANES), F32)],
        0,
    )


def full_batch(picked, template, src_ref):
    arm = arms_of(picked, template)
    weight = 10.0 + 10.0 * picked[0:MEMBERS]
    tail = jnp.zeros((8, LANES), F32)
    margins = []
    for cut in (slice(0, HALF), slice(HALF, MEMBERS)):
        own = [a[cut] for a in arm]
        place = [picked[POS + k : POS + k + 1] + own[k] for k in range(3)]
        out = contact(place, weight[cut], src_ref)
        margins.append(out[3])
        tail = tail + body_rows(own, out[0:3])
    return jnp.concatenate(margins + [tail], 0)


def half_batch(picked, template, src_ref):
    arm = arms_of(picked, [halves(t) for t in template])
    weight = 10.0 + 10.0 * halves(picked[0:MEMBERS])
    place = [picked[POS + k : POS + k + 1] + arm[k] for k in range(3)]
    out = contact(place, weight, src_ref)
    lane = lax.broadcasted_iota(I32, (HALF, LANES), 1)
    lower = jnp.where(lane < PAIRS, out[3], 0.0)
    upper = jnp.where(lane < PAIRS, 0.0, out[3])
    return jnp.concatenate([lower, upper, body_rows(arm, out[0:3])], 0)


def pack_kernel(pos_ref, ori_ref, hist_ref, local_ref, ghost_ref, count_ref, out_ref):
    out_ref[0:MEMBERS] = hist_ref[...]
    slot = lax.broadcasted_iota(I32, (1, PAIRS), 1)
    live = slot < count_ref[0]
    local = local_ref[...].astype(F32)
    code = jnp.where(live, ghost_ref[...], ghost_ref[...] + IDLE).astype(F32)
    lists = jnp.concatenate([local, local, code, code], 1)
    out_ref[MEMBERS:PACKED] = jnp.concatenate([pos_ref[...], ori_ref[...], lists], 0)


def inner_kernel(packed_ref, template_ref, first_ref, gap_ref, out_ref, src_ref):
    template = spread_template(template_ref)
    first = first_ref[...]
    second = jnp.bitwise_and(first + gap_ref[...], CLUMPS - 1)
    target = one_hot(jnp.concatenate([first, second], 1))
    source = one_hot(jnp.concatenate([second, first], 1))
    parts = parts_of(packed_ref[...])
    picked = gather(parts, source)
    place_source(src_ref, picked, arms_of(picked, template), (0.0, 0.0, 0.0))
    rows = full_batch(gather(parts, target), template, src_ref)
    out_ref[...] = scatter(rows, target)


def outer_kernel(
    packed_ref,
    brick_next_ref,
    slab_next_ref,
    brick_back_ref,
    slab_back_ref,
    inner_ref,
    velocity_ref,
    template_ref,
    local_ref,
    ghost_ref,
    count_ref,
    leaving_ref,
    leaving_row_ref,
    target_ref,
    target_row_ref,
    staying_ref,
    buffer_ref,
    src_ref,
):
    template = spread_template(template_ref)
    lane = lax.broadcasted_iota(I32, (1, LANES), 1)
    low = lane < PAIRS
    local = local_ref[...]
    ghost = ghost_ref[...]
    live = lax.broadcasted_iota(I32, (1, PAIRS), 1) < count_ref[0]
    local_code = jnp.where(live, local, local + IDLE)
    local = jnp.concatenate([local, local], 1)
    ghost = jnp.concatenate([ghost, ghost], 1)
    local_code = jnp.concatenate([local_code, local_code], 1)
    brick_lists = brick_back_ref[LISTS : LISTS + 1].astype(I32)
    slab_lists = slab_back_ref[LISTS : LISTS + 1].astype(I32)
    brick_local, brick_code = brick_lists[:, :LANES], brick_lists[:, LANES:]
    slab_local, slab_code = slab_lists[:, :LANES], slab_lists[:, LANES:]

    own = parts_of(packed_ref[...])
    source = (
        gather(parts_of(brick_next_ref[...]), one_hot(jnp.where(low, ghost, -1)))
        + gather(parts_of(slab_next_ref[...]), one_hot(jnp.where(low, ghost - CLUMPS, -1)))
        + gather(parts_of(brick_back_ref[...]), one_hot(jnp.where(low, -1, brick_local)))
    )
    near = ghost < CLUMPS
    shift = (
        jnp.where(low, jnp.where(near, 0.0, 1.0), 0.0),
        jnp.where(low, jnp.where(near, 1.0, 0.0), -1.0),
        0.0,
    )
    place_source(src_ref, source, arms_of(source, template), shift)
    chosen = one_hot(jnp.where(low, local, jnp.bitwise_and(brick_code, CLUMPS - 1)))
    rows = full_batch(gather(own, chosen), template, src_ref)
    totals = inner_ref[...] + scatter(rows, one_hot(jnp.where(low, local_code, brick_code)))

    source = gather(parts_of(slab_back_ref[...]), one_hot(slab_local))
    place_source(src_ref, source, arms_of(source, template), (-1.0, 0.0, 0.0))
    chosen = one_hot(jnp.bitwise_and(slab_code, CLUMPS - 1))
    rows = half_batch(gather(own, chosen), template, src_ref)
    totals = totals + scatter(rows, one_hot(slab_code - CLUMPS))

    state = packed_ref[...]
    velocity = velocity_ref[...]
    orient = [state[ORI + k : ORI + k + 1] for k in range(4)]
    force = totals[MEMBERS : MEMBERS + 3]
    torque = totals[MEMBERS + 3 : MEMBERS + 6]
    linear = velocity[0:3] + TIME_STEP * force
    angular = velocity[3:6] + TIME_STEP * torque / INERTIA_SCALE
    centre = state[POS : POS + 3] + TIME_STEP * linear
    wx, wy, wz = [angular[k : k + 1] for k in range(3)]
    ow, ox, oy, oz = orient
    spin = [
        -(wx * ox + wy * oy + wz * oz),
        ow * wx + (wy * oz - wz * oy),
        ow * wy + (wz * ox - wx * oz),
        ow * wz + (wx * oy - wy * ox),
    ]
    turned = [orient[k] + 0.5 * TIME_STEP * spin[k] for k in range(4)]
    history = HISTORY_DECAY * state[0:MEMBERS] + totals[0:MEMBERS]
    head = jnp.concatenate([centre] + turned + [linear, angular], 0)

    dest = target_row_ref[...]
    order = lax.broadcasted_iota(I32, (PAIRS, PAIRS), 0) < lax.broadcasted_iota(I32, (PAIRS, PAIRS), 1)
    same = jnp.where(order & (target_ref[...] == dest), 1.0, 0.0)
    rank = jnp.sum(same, axis=0, keepdims=True).astype(I32)
    column = one_hot(dest * SLOT_CAP + rank, 64 * SLOT_CAP)
    clump = lax.broadcasted_iota(I32, (PAIRS, CLUMPS), 1)
    leaves = jnp.where(leaving_ref[...] == clump, 1.0, 0.0)
    departed = jnp.sum(leaves, axis=0, keepdims=True) > 0.5
    route = jnp.dot(column, leaves.astype(BF16), preferred_element_type=F32).astype(BF16)
    full = jnp.concatenate([history, head, jnp.zeros((LANES - 77, CLUMPS), F32)], 0)
    buffer_ref[...] = sum(
        lax.dot_general(route, part, (((1,), (1,)), ((), ())), preferred_element_type=F32)
        for part in parts_of(full)
    )
    staying_ref[0:13] = jnp.where(departed, 0.0, head)
    staying_ref[13:77] = jnp.where(departed, 0.0, history)


def turn_kernel(in_ref, out_ref):
    turned = in_ref[...].T
    out_ref[0:13] = turned[MEMBERS : MEMBERS + 13]
    out_ref[13:77] = turned[0:MEMBERS]


def vmem():
    return pl.BlockSpec(memory_space=pltpu.VMEM)


def smem():
    return pl.BlockSpec(memory_space=pltpu.SMEM)


def from_behind(value, axis, steps):
    count = lax.axis_size(axis)
    pairs = [(source, (source + steps) % count) for source in range(count)]
    return lax.ppermute(value, axis, pairs)


def shards(
    position,
    orient,
    velocity,
    history,
    template,
    cross_local,
    cross_ghost,
    cross_count,
    inner_first,
    inner_gap,
    mig_index,
    mig_dest,
):
    row = (1, PAIRS)
    local, ghost = cross_local.reshape(row), cross_ghost.reshape(row)
    packed = pl.pallas_call(
        pack_kernel,
        out_shape=jax.ShapeDtypeStruct((PACKED, CLUMPS), F32),
        in_specs=[vmem()] * 5 + [smem()],
        out_specs=vmem(),
        name="pack",
    )(position, orient, history, local, ghost, cross_count)
    slab_next = from_behind(packed, "slab", -1)
    slab_back = from_behind(packed, "slab", 1)
    brick_next = from_behind(packed, "brick", -1)
    brick_back = from_behind(packed, "brick", 1)
    inner = pl.pallas_call(
        inner_kernel,
        out_shape=jax.ShapeDtypeStruct((PACKED, CLUMPS), F32),
        in_specs=[vmem()] * 4,
        out_specs=vmem(),
        scratch_shapes=[pltpu.VMEM((4, MEMBERS, LANES), F32)],
        cost_estimate=pl.CostEstimate(flops=20_000_000, bytes_accessed=400_000, transcendentals=600_000),
        name="inner",
    )(packed, template, inner_first.reshape(row), inner_gap.reshape(row))
    staying, buffer = pl.pallas_call(
        outer_kernel,
        out_shape=(
            jax.ShapeDtypeStruct((77, CLUMPS), F32),
            jax.ShapeDtypeStruct((64 * SLOT_CAP, LANES), F32),
        ),
        in_specs=[vmem()] * 10 + [smem()] + [vmem()] * 4,
        out_specs=(vmem(), vmem()),
        scratch_shapes=[pltpu.VMEM((4, MEMBERS, LANES), F32)],
        cost_estimate=pl.CostEstimate(flops=30_000_000, bytes_accessed=400_000, transcendentals=800_000),
        name="outer",
    )(
        packed,
        brick_next,
        slab_next,
        brick_back,
        slab_back,
        inner,
        velocity,
        template,
        local,
        ghost,
        cross_count,
        mig_index.reshape(PAIRS, 1),
        mig_index.reshape(row),
        mig_dest,
        mig_dest.reshape(row),
    )
    arrived = lax.all_to_all(buffer.reshape(64, SLOT_CAP, LANES), "brick", split_axis=0, concat_axis=0)
    arrivals = pl.pallas_call(
        turn_kernel,
        out_shape=jax.ShapeDtypeStruct((77, 64 * SLOT_CAP), F32),
        in_specs=[vmem()],
        out_specs=vmem(),
        name="turn",
    )(arrived.reshape(64 * SLOT_CAP, LANES))
    return (staying, arrivals)


def solution(mesh):
    both = ("slab", "brick")
    return jax.shard_map(
        shards,
        mesh=mesh,
        in_specs=(
            P(None, both),
            P(None, both),
            P(None, both),
            P(None, both),
            P(),
            P(both),
            P(both),
            P(both),
            P(both),
            P(both),
            P(both),
            P(both, None),
        ),
        out_specs=(P(None, both), P(None, both)),
        check_vma=False,
    )
```

time: 78.6 us -> 54.3 us (0.69)
  blocking collectives: 0 us -> 19.9 us
  waiting for transfers between devices: 19.6 us -> 0.01 us
  other arithmetic: 18.5 us -> 0 us
  local copies, waits for them, and re-layouts: 15.8 us -> 2.07 us
  Pallas kernels: 0 us -> 12.9 us
  starting transfers between devices: 21.1 us -> 17.5 us
    all_to_all x0 -> x1, blocking collectives: none -> 19.9 us  [shards(): lax.all_to_all(buffer.reshape(64, SLOT_CAP, LANES), 'brick', split_axis=0...]
    pallas_call x0 -> x4, Pallas kernels: none -> 12.9 us  [the longest x1 5.79 us: shards(): pl.pallas_call(outer_kernel, out_shape=(jax.ShapeDtypeStruct((77, CLUMPS)...]
    all_to_all x1 -> x0, waiting for transfers between devices: 11.7 us -> none  [shards(): lax.all_to_all(buffer, 'brick', split_axis=1, concat_axis=1, tiled=True)]
    reduce_sum x13 -> x0, other arithmetic: 9.87 us -> none  [the longest x2 3.39 us: contact_block(): jnp.sum(margin, 1)]
    gather x25 -> x0, local copies, waits for them, and re-layouts: 9.11 us -> none  [the longest x4 1.53 us: accumulate(): arm_b_all[:, :, sel_b]]
    ppermute x4, waiting for transfers between devices: 8 us -> 0.01 us  [from_behind(): return lax.ppermute(value, axis, pairs)]
    all_to_all x1 -> x0, starting transfers between devices: 5.09 us -> none  [shards(): lax.all_to_all(buffer, 'brick', split_axis=1, concat_axis=1, tiled=True)]
    select_n x5 -> x0, other arithmetic: 2.11 us -> none  [the longest x1 0.69 us: accumulate(): totals_now[0].at[:, sel_a].add(row_a)]
  transfers between devices with their start and end apart: 5 -> 4, of which waited for: 3 -> 0; matrix products, arithmetic and copies ran while one was open for 21% -> 3% of each run, Pallas kernels for 0% -> 7%
where the time goes in v1:
time: 54.3 us; the launch traced here: 53.8 us
  blocking collectives  19.9 us (37%)
  starting transfers between devices  17.5 us (32%)
  Pallas kernels  12.9 us (24%)
  local copies, waits for them, and re-layouts  2.07 us (4%)
  between operations  1.36 us (3%)
    all_to_all x1, blocking collectives, shards(): lax.all_to_all(buffer.reshape(64, SLOT_CAP, LANES), 'brick', split_axis=0...  19.9 us
    ppermute x4, starting transfers between devices, from_behind(): return lax.ppermute(value, axis, pairs)  17.5 us
    pallas_call x1, Pallas kernels, shards(): pl.pallas_call(outer_kernel, out_shape=(jax.ShapeDtypeStruct((77, CLUMPS)...  5.79 us
    pallas_call x1, Pallas kernels, shards(): pl.pallas_call(inner_kernel, out_shape=jax.ShapeDtypeStruct((PACKED, CLUM...  3.97 us
    pallas_call x1, Pallas kernels, shards(): pl.pallas_call(pack_kernel, out_shape=jax.ShapeDtypeStruct((PACKED, CLUMP...  1.59 us
    pallas_call x1, Pallas kernels, shards(): pl.pallas_call(turn_kernel, out_shape=jax.ShapeDtypeStruct((77, 64 * SLOT...  1.54 us
    unnamed x13, local copies, waits for them, and re-layouts  1.36 us
  transfers between devices with their start and end apart: 4, of which 0 were waited for; matrix products, arithmetic and copies ran while one was open for 3% of the time, Pallas kernels for 7%

profile of v1, /device:TPU:6, one launch (start us, length us, event | category | flops | bytes accessed | tf_op | source)
XLA Modules:
  0.0 53.8 jit_solution(3843710293366917219)
XLA Ops:
  1.3 1.6 %pack.1.packed_ref = f32[72,256]{1,0:T(8,128)} custom-call(f32[3,256]{1,0:T(4,128)} %pos_ref.1, f32[4,256]{1,0:T(4,128)} %ori_ref.1, f32[64,256]{1,0:T(8,128)} %hist_ref.1, s32[1,64]{1,0:T(1,128)} %bitcast.11, s32[1,64]{1,0:T(1,128)} %bitcast.13, s32[1]{0:T(128)S(6)} %copy.16.count_ref), custom_call_target="tpu_custom_call" | custom-call | tf_op jit(solution)/shard_map/pack/pallas_call | solution.py:296
  2.9 0.0 copy-start
  2.9 0.0 collective-permute-start.3
  2.9 4.4 %collective-permute-start.2 = (f32[72,256]{1,0:T(8,128)}, f32[72,256]{1,0:T(8,128)S(1)}, u32[]{:S(2)}, u32[]{:S(2)}) collective-permute-start(f32[72,256]{1,0:T(8,128)} %pack.1.packed_ref), channel_id=1, source_target_pairs={{0,1},{1,2},{2,3},{3,4},{4,5},{5,6},{6,7},{7,8},{8,9},{9,10},{10,1... | collective-permute-start | bytes 221192 | tf_op jit(solution)/shard_map/ppermute | solution.py:277
  7.3 1.3 %collective-permute-start.1 = (f32[72,256]{1,0:T(8,128)}, f32[72,256]{1,0:T(8,128)S(1)}, u32[]{:S(2)}, u32[]{:S(2)}) collective-permute-start(f32[72,256]{1,0:T(8,128)} %pack.1.packed_ref), channel_id=1, source_target_pairs={{0,448},{64,0},{128,64},{192,128},{256,192},{320,256},{384,320},{4... | collective-permute-start | bytes 221192 | tf_op jit(solution)/shard_map/ppermute | solution.py:277
  8.6 11.8 %collective-permute-start = (f32[72,256]{1,0:T(8,128)}, f32[72,256]{1,0:T(8,128)S(1)}, u32[]{:S(2)}, u32[]{:S(2)}) collective-permute-start(f32[72,256]{1,0:T(8,128)} %pack.1.packed_ref), channel_id=1, source_target_pairs={{0,63},{1,0},{2,1},{3,2},{4,3},{5,4},{6,5},{7,6},{8,7},{9,8},{10,9... | collective-permute-start | bytes 221192 | tf_op jit(solution)/shard_map/ppermute | solution.py:277
  20.4 0.0 copy-done
  20.4 0.0 copy-start.1
  20.4 0.7 %copy.14.leaving_ref = s32[64,1]{1,0:T(8,128)} copy(s32[64,1]{0,1:T(1,128)S(1)} %bitcast.16) | data formatting | bytes 512 | tf_op jit(solution)/shard_map/reshape | solution.py:339
  21.1 0.0 copy-done.1
  21.1 0.7 %copy.15.target_ref = s32[64,1]{1,0:T(8,128)} copy(s32[64,1]{0,1:T(1,128)S(1)} %copy-done.1) | data formatting | bytes 512 | tf_op args[11]
  21.8 4.0 %inner.1.inner_ref = f32[72,256]{1,0:T(8,128)} custom-call(f32[72,256]{1,0:T(8,128)} %pack.1.packed_ref, f32[3,64]{1,0:T(4,128)} %template_ref.3, s32[1,64]{1,0:T(1,128)} %bitcast.18, s32[1,64]{1,0:T(1,128)} %bitcast.19), custom_call_target="tpu_custom_call" | custom-call | flops 20000000 | bytes 400000 | tf_op jit(solution)/shard_map/inner/pallas_call | solution.py:307
  25.8 0.0 collective-permute-done.3.slab_back_ref
  25.8 0.0 copy-start.2
  25.8 0.0 collective-permute-done.2.brick_back_ref
  25.8 0.0 copy-start.3
  25.8 0.0 collective-permute-done.1.slab_next_ref
  25.8 0.0 copy-start.4
  25.8 0.0 collective-permute-done.brick_next_ref
  25.9 0.0 copy-start.5
  25.9 0.6 %copy-done.2 = f32[72,256]{1,0:T(8,128)} copy-done((f32[72,256]{1,0:T(8,128)}, f32[72,256]{1,0:T(8,128)S(1)}, u32[]{:S(2)}) %copy-start.2) | copy-done | bytes 73752
  26.4 0.0 copy-done.3
  26.5 0.0 copy-done.4
  26.5 0.0 copy-done.5
  26.5 5.8 %outer.1 = (f32[77,256]{1,0:T(8,128)}, f32[128,128]{1,0:T(8,128)}) custom-call(f32[72,256]{1,0:T(8,128)} %pack.1.packed_ref, f32[72,256]{1,0:T(8,128)} %copy-done.5, f32[72,256]{1,0:T(8,128)} %copy-done.4, f32[72,256]{1,0:T(8,128)} %copy-done.3, f32[72,256]{1,0:T(8,128)} %copy-done.2, f32[72,256]{1,0:T(8,128)} %inner.1.inner_ref, f32[6,256]{1,0:T(8,128)} %velocity_ref.1, ...), custom_call_target="tpu_custom_call" | custom-call | flops 30000000 | bytes 400000 | tf_op jit(solution)/shard_map/outer/pallas_call | solution.py:316
  32.3 19.9 %all_to_all.5 = f32[64,2,128]{2,1,0:T(2,128)} all-to-all(f32[64,2,128]{2,1,0:T(2,128)} %bitcast.10), channel_id=1, replica_groups=mesh['slab'=8,'brick'=64] {'brick'}, dimensions={0} | all-to-all | bytes 131072 | tf_op jit(solution)/shard_map/all_to_all | solution.py:344
  52.2 1.5 %turn.1 = f32[77,128]{1,0:T(8,128)} custom-call(f32[128,128]{1,0:T(8,128)} %bitcast.9), custom_call_target="tpu_custom_call" | custom-call | tf_op jit(solution)/shard_map/turn/pallas_call | solution.py:345
Async XLA Ops:
  2.9 17.5 %copy-start = (s32[64]{0:T(128)S(1)}, s32[64]{0:T(128)}, u32[]{:S(2)}) copy-start(s32[64]{0:T(128)} %param.22) | copy-start | bytes 772
  2.9 22.9 %collective-permute-start.3 = (f32[72,256]{1,0:T(8,128)}, f32[72,256]{1,0:T(8,128)S(1)}, u32[]{:S(2)}, u32[]{:S(2)}) collective-permute-start(f32[72,256]{1,0:T(8,128)} %pack.1.packed_ref), channel_id=1, source_target_pairs={{0,64},{64,128},{128,192},{192,256},{256,320},{320,384},{384,448},... | collective-permute-start | bytes 221192 | tf_op jit(solution)/shard_map/ppermute | solution.py:277
  2.9 22.9 %collective-permute-start.2 = (f32[72,256]{1,0:T(8,128)}, f32[72,256]{1,0:T(8,128)S(1)}, u32[]{:S(2)}, u32[]{:S(2)}) collective-permute-start(f32[72,256]{1,0:T(8,128)} %pack.1.packed_ref), channel_id=1, source_target_pairs={{0,1},{1,2},{2,3},{3,4},{4,5},{5,6},{6,7},{7,8},{8,9},{9,10},{10,1... | collective-permute-start | bytes 221192 | tf_op jit(solution)/shard_map/ppermute | solution.py:277
  7.3 18.5 %collective-permute-start.1 = (f32[72,256]{1,0:T(8,128)}, f32[72,256]{1,0:T(8,128)S(1)}, u32[]{:S(2)}, u32[]{:S(2)}) collective-permute-start(f32[72,256]{1,0:T(8,128)} %pack.1.packed_ref), channel_id=1, source_target_pairs={{0,448},{64,0},{128,64},{192,128},{256,192},{320,256},{384,320},{4... | collective-permute-start | bytes 221192 | tf_op jit(solution)/shard_map/ppermute | solution.py:277
  8.6 17.2 %collective-permute-start = (f32[72,256]{1,0:T(8,128)}, f32[72,256]{1,0:T(8,128)S(1)}, u32[]{:S(2)}, u32[]{:S(2)}) collective-permute-start(f32[72,256]{1,0:T(8,128)} %pack.1.packed_ref), channel_id=1, source_target_pairs={{0,63},{1,0},{2,1},{3,2},{4,3},{5,4},{6,5},{7,6},{8,7},{9,8},{10,9... | collective-permute-start | bytes 221192 | tf_op jit(solution)/shard_map/ppermute | solution.py:277
  20.4 0.7 %copy-start.1 = (s32[64,1]{0,1:T(1,128)S(1)}, s32[64,1]{0,1:T(1,128)}, u32[]{:S(2)}) copy-start(s32[64,1]{0,1:T(1,128)} %param.23) | copy-start | bytes 772
  25.8 0.6 %copy-start.2 = (f32[72,256]{1,0:T(8,128)}, f32[72,256]{1,0:T(8,128)S(1)}, u32[]{:S(2)}) copy-start(f32[72,256]{1,0:T(8,128)S(1)} %collective-permute-done.3.slab_back_ref) | copy-start | bytes 221188
  25.8 0.6 %copy-start.3 = (f32[72,256]{1,0:T(8,128)}, f32[72,256]{1,0:T(8,128)S(1)}, u32[]{:S(2)}) copy-start(f32[72,256]{1,0:T(8,128)S(1)} %collective-permute-done.2.brick_back_ref) | copy-start | bytes 221188
  25.8 0.6 %copy-start.4 = (f32[72,256]{1,0:T(8,128)}, f32[72,256]{1,0:T(8,128)S(1)}, u32[]{:S(2)}) copy-start(f32[72,256]{1,0:T(8,128)S(1)} %collective-permute-done.1.slab_next_ref) | copy-start | bytes 221188
  25.9 0.6 %copy-start.5 = (f32[72,256]{1,0:T(8,128)}, f32[72,256]{1,0:T(8,128)S(1)}, u32[]{:S(2)}) copy-start(f32[72,256]{1,0:T(8,128)S(1)} %collective-permute-done.brick_next_ref) | copy-start | bytes 221188

commit v2 on v1

--- a/solution.py
+++ b/solution.py
@@ -11,6 +11,7 @@
 PAIRS = 64
 HALF = MEMBERS // 2
 SLOT_CAP = 2
+VMEM_LIMIT = 4 * 1024 * 1024
 IDLE = 1024
 
 DIAMETER = 0.3
@@ -148,7 +149,33 @@
     out_ref[MEMBERS:PACKED] = jnp.concatenate([pos_ref[...], ori_ref[...], lists], 0)
 
 
-def inner_kernel(packed_ref, template_ref, first_ref, gap_ref, out_ref, src_ref):
+def routes(leaving, dest):
+    to = one_hot(dest, 64)
+    before = lax.broadcasted_iota(I32, (PAIRS, PAIRS), 0) < lax.broadcasted_iota(I32, (PAIRS, PAIRS), 1)
+    before = jnp.where(before, 1.0, 0.0).astype(BF16)
+    earlier = jnp.dot(to, before, preferred_element_type=F32)
+    rank = jnp.sum(earlier * to.astype(F32), axis=0, keepdims=True).astype(I32)
+    column = one_hot(dest * SLOT_CAP + rank, 64 * SLOT_CAP)
+    leaves = one_hot(leaving)
+    dims = (((1,), (1,)), ((), ()))
+    route = lax.dot_general(column, leaves, dims, preferred_element_type=F32)
+    ones = jnp.ones((8, PAIRS), F32).astype(BF16)
+    return route, lax.dot_general(ones, leaves, dims, preferred_element_type=F32)
+
+
+def inner_kernel(
+    packed_ref,
+    template_ref,
+    first_ref,
+    gap_ref,
+    leaving_ref,
+    dest_ref,
+    out_ref,
+    route_ref,
+    departed_ref,
+    src_ref,
+):
+    route_ref[...], departed_ref[...] = routes(leaving_ref[...], dest_ref[...])
     template = spread_template(template_ref)
     first = first_ref[...]
     second = jnp.bitwise_and(first + gap_ref[...], CLUMPS - 1)
@@ -173,10 +200,8 @@
     local_ref,
     ghost_ref,
     count_ref,
-    leaving_ref,
-    leaving_row_ref,
-    target_ref,
-    target_row_ref,
+    route_ref,
+    departed_ref,
     staying_ref,
     buffer_ref,
     src_ref,
@@ -239,15 +264,8 @@
     history = HISTORY_DECAY * state[0:MEMBERS] + totals[0:MEMBERS]
     head = jnp.concatenate([centre] + turned + [linear, angular], 0)
 
-    dest = target_row_ref[...]
-    order = lax.broadcasted_iota(I32, (PAIRS, PAIRS), 0) < lax.broadcasted_iota(I32, (PAIRS, PAIRS), 1)
-    same = jnp.where(order & (target_ref[...] == dest), 1.0, 0.0)
-    rank = jnp.sum(same, axis=0, keepdims=True).astype(I32)
-    column = one_hot(dest * SLOT_CAP + rank, 64 * SLOT_CAP)
-    clump = lax.broadcasted_iota(I32, (PAIRS, CLUMPS), 1)
-    leaves = jnp.where(leaving_ref[...] == clump, 1.0, 0.0)
-    departed = jnp.sum(leaves, axis=0, keepdims=True) > 0.5
-    route = jnp.dot(column, leaves.astype(BF16), preferred_element_type=F32).astype(BF16)
+    departed = departed_ref[0:1] > 0.5
+    route = route_ref[...].astype(BF16)
     full = jnp.concatenate([history, head, jnp.zeros((LANES - 77, CLUMPS), F32)], 0)
     buffer_ref[...] = sum(
         lax.dot_general(route, part, (((1,), (1,)), ((), ())), preferred_element_type=F32)
@@ -265,6 +283,10 @@
 
 def vmem():
     return pl.BlockSpec(memory_space=pltpu.VMEM)
+
+
+def small():
+    return pltpu.CompilerParams(vmem_limit_bytes=VMEM_LIMIT)
 
 
 def smem():
@@ -298,31 +320,45 @@
         out_shape=jax.ShapeDtypeStruct((PACKED, CLUMPS), F32),
         in_specs=[vmem()] * 5 + [smem()],
         out_specs=vmem(),
+        compiler_params=small(),
         name="pack",
     )(position, orient, history, local, ghost, cross_count)
     slab_next = from_behind(packed, "slab", -1)
     slab_back = from_behind(packed, "slab", 1)
     brick_next = from_behind(packed, "brick", -1)
     brick_back = from_behind(packed, "brick", 1)
-    inner = pl.pallas_call(
+    inner, route, departed = pl.pallas_call(
         inner_kernel,
-        out_shape=jax.ShapeDtypeStruct((PACKED, CLUMPS), F32),
-        in_specs=[vmem()] * 4,
-        out_specs=vmem(),
+        out_shape=(
+            jax.ShapeDtypeStruct((PACKED, CLUMPS), F32),
+            jax.ShapeDtypeStruct((64 * SLOT_CAP, CLUMPS), F32),
+            jax.ShapeDtypeStruct((8, CLUMPS), F32),
+        ),
+        in_specs=[vmem()] * 6,
+        out_specs=(vmem(),) * 3,
         scratch_shapes=[pltpu.VMEM((4, MEMBERS, LANES), F32)],
         cost_estimate=pl.CostEstimate(flops=20_000_000, bytes_accessed=400_000, transcendentals=600_000),
+        compiler_params=small(),
         name="inner",
-    )(packed, template, inner_first.reshape(row), inner_gap.reshape(row))
+    )(
+        packed,
+        template,
+        inner_first.reshape(row),
+        inner_gap.reshape(row),
+        mig_index.reshape(row),
+        mig_dest.reshape(row),
+    )
     staying, buffer = pl.pallas_call(
         outer_kernel,
         out_shape=(
             jax.ShapeDtypeStruct((77, CLUMPS), F32),
             jax.ShapeDtypeStruct((64 * SLOT_CAP, LANES), F32),
         ),
-        in_specs=[vmem()] * 10 + [smem()] + [vmem()] * 4,
+        in_specs=[vmem()] * 10 + [smem()] + [vmem()] * 2,
         out_specs=(vmem(), vmem()),
         scratch_shapes=[pltpu.VMEM((4, MEMBERS, LANES), F32)],
         cost_estimate=pl.CostEstimate(flops=30_000_000, bytes_accessed=400_000, transcendentals=800_000),
+        compiler_params=small(),
         name="outer",
     )(
         packed,
@@ -336,10 +372,8 @@
         local,
         ghost,
         cross_count,
-        mig_index.reshape(PAIRS, 1),
-        mig_index.reshape(row),
-        mig_dest,
-        mig_dest.reshape(row),
+        route,
+        departed,
     )
     arrived = lax.all_to_all(buffer.reshape(64, SLOT_CAP, LANES), "brick", split_axis=0, concat_axis=0)
     arrivals = pl.pallas_call(
@@ -347,6 +381,7 @@
         out_shape=jax.ShapeDtypeStruct((77, 64 * SLOT_CAP), F32),
         in_specs=[vmem()],
         out_specs=vmem(),
+        compiler_params=small(),
         name="turn",
     )(arrived.reshape(64 * SLOT_CAP, LANES))
     return (staying, arrivals)

time: 54.3 us -> 50 us (0.921)
  Pallas kernels: 12.9 us -> 7.85 us
  local copies, waits for them, and re-layouts: 2.07 us -> 2.86 us
    pallas_call x1, Pallas kernels: 1.59 us -> 0.08 us  [shards(): pl.pallas_call(pack_kernel, out_shape=jax.ShapeDtypeStruct((PACKED, CLUMP...]
    unnamed x13 -> x22, local copies, waits for them, and re-layouts: 1.36 us -> 2.86 us
    pallas_call x1, Pallas kernels: 3.97 us -> 2.56 us  [shards(): pl.pallas_call(inner_kernel, out_shape=(jax.ShapeDtypeStruct((PACKED, CLU...]
    pallas_call x1, Pallas kernels: 5.79 us -> 4.5 us  [shards(): pl.pallas_call(outer_kernel, out_shape=(jax.ShapeDtypeStruct((77, CLUMPS)...]
    pallas_call x1, Pallas kernels: 1.54 us -> 0.7 us  [shards(): pl.pallas_call(turn_kernel, out_shape=jax.ShapeDtypeStruct((77, 64 * SLOT...]
    reshape x1 -> x0, local copies, waits for them, and re-layouts: 0.71 us -> none  [shards(): mig_index.reshape(PAIRS, 1)]
  transfers between devices with their start and end apart: 4 -> 4, of which waited for: 0 -> 0; matrix products, arithmetic and copies ran while one was open for 3% -> 0% of each run, Pallas kernels for 7% -> 5%
where the time goes in v2:
time: 50 us; the launch traced here: 49.4 us
  blocking collectives  19.8 us (40%)
  starting transfers between devices  17.5 us (35%)
  Pallas kernels  7.85 us (16%)
  local copies, waits for them, and re-layouts  2.86 us (6%)
  between operations  1.43 us (3%)
    all_to_all x1, blocking collectives, shards(): lax.all_to_all(buffer.reshape(64, SLOT_CAP, LANES), 'brick', split_axis=0...  19.8 us
    ppermute x4, starting transfers between devices, from_behind(): return lax.ppermute(value, axis, pairs)  17.5 us
    pallas_call x1, Pallas kernels, shards(): pl.pallas_call(outer_kernel, out_shape=(jax.ShapeDtypeStruct((77, CLUMPS)...  4.5 us
    unnamed x22, local copies, waits for them, and re-layouts  2.86 us
    pallas_call x1, Pallas kernels, shards(): pl.pallas_call(inner_kernel, out_shape=(jax.ShapeDtypeStruct((PACKED, CLU...  2.56 us
  transfers between devices with their start and end apart: 4, of which 0 were waited for; matrix products, arithmetic and copies ran while one was open for 0% of the time, Pallas kernels for 5%

profile of v2, /device:TPU:6, one launch (start us, length us, event | category | flops | bytes accessed | tf_op | source)
XLA Modules:
  0.0 49.4 jit_solution(16922451306466977612)
XLA Ops:
  0.6 0.0 copy-start.1
  1.3 0.0 copy-start.3
  1.3 0.0 copy-start.4
  1.3 0.0 copy-done.1
  1.3 0.6 %copy-done.3 = s32[64]{0:T(128)S(1)} copy-done((s32[64]{0:T(128)S(1)}, s32[64]{0:T(128)}, u32[]{:S(2)}) %copy-start.3) | copy-done | bytes 280
  2.0 0.0 copy-done.4
  2.0 0.0 copy-start
  2.0 0.8 %copy-done = f32[64,256]{1,0:T(8,128)S(1)} copy-done((f32[64,256]{1,0:T(8,128)S(1)}, f32[64,256]{1,0:T(8,128)}, u32[]{:S(2)}) %copy-start) | copy-done | bytes 65560
  2.8 0.0 copy-start.2
  2.8 0.7 %copy-done.2 = f32[4,256]{1,0:T(4,128)S(1)} copy-done((f32[4,256]{1,0:T(4,128)S(1)}, f32[4,256]{1,0:T(4,128)}, u32[]{:S(2)}) %copy-start.2) | copy-done | bytes 4120
  3.5 0.1 pack.1.packed_ref
  3.6 0.0 collective-permute-start.3
  3.6 4.3 %collective-permute-start.2 = (f32[72,256]{1,0:T(8,128)S(1)}, f32[72,256]{1,0:T(8,128)S(1)}, u32[]{:S(2)}, u32[]{:S(2)}) collective-permute-start(f32[72,256]{1,0:T(8,128)S(1)} %pack.1.packed_ref), channel_id=1, source_target_pairs={{0,1},{1,2},{2,3},{3,4},{4,5},{5,6},{6,7},{7,8},{8,9},{9,10},{10,1... | collective-permute-start | bytes 221192 | tf_op jit(solution)/shard_map/ppermute | solution.py:299
  7.9 1.5 %collective-permute-start.1 = (f32[72,256]{1,0:T(8,128)S(1)}, f32[72,256]{1,0:T(8,128)S(1)}, u32[]{:S(2)}, u32[]{:S(2)}) collective-permute-start(f32[72,256]{1,0:T(8,128)S(1)} %pack.1.packed_ref), channel_id=1, source_target_pairs={{0,448},{64,0},{128,64},{192,128},{256,192},{320,256},{384,320},{4... | collective-permute-start | bytes 221192 | tf_op jit(solution)/shard_map/ppermute | solution.py:299
  9.3 11.8 %collective-permute-start = (f32[72,256]{1,0:T(8,128)S(1)}, f32[72,256]{1,0:T(8,128)S(1)}, u32[]{:S(2)}, u32[]{:S(2)}) collective-permute-start(f32[72,256]{1,0:T(8,128)S(1)} %pack.1.packed_ref), channel_id=1, source_target_pairs={{0,63},{1,0},{2,1},{3,2},{4,3},{5,4},{6,5},{7,6},{8,7},{9,8},{10,9... | collective-permute-start | bytes 221192 | tf_op jit(solution)/shard_map/ppermute | solution.py:299
  21.1 0.0 copy-start.10
  21.1 0.0 copy-start.6
  21.1 0.0 copy-start.7
  21.1 0.0 copy-start.8
  21.1 0.0 copy-start.9
  21.2 0.6 %copy-done.10 = s32[64,1]{0,1:T(1,128)S(1)} copy-done((s32[64,1]{0,1:T(1,128)S(1)}, s32[64,1]{0,1:T(1,128)}, u32[]{:S(2)}) %copy-start.10) | copy-done | bytes 280
  21.8 0.0 copy-done.6
  21.8 0.0 copy-done.7
  21.8 0.0 copy-done.8
  21.8 0.0 copy-done.9
  21.8 0.0 copy-start.5
  21.8 2.6 %inner.1 = (f32[72,256]{1,0:T(8,128)S(1)}, f32[128,256]{1,0:T(8,128)S(1)}, f32[8,256]{1,0:T(8,128)S(1)}) custom-call(f32[72,256]{1,0:T(8,128)S(1)} %pack.1.packed_ref, f32[3,64]{1,0:T(4,128)S(1)} %copy-done.6, s32[1,64]{1,0:T(1,128)S(1)} %bitcast.14, s32[1,64]{1,0:T(1,128)S(1)} %bitcast.15, s32[1,64]{1,0:T(1,128)S(1)} %bitcast.16, s32[1,64]{1,0:T(1,128)S(1)} %bitcast.17), custom_call_target="tpu_custom_call" | custom-call | flops 20000000 | bytes 400000 | tf_op jit(solution)/shard_map/inner/pallas_call | solution.py:330
  24.4 0.0 collective-permute-done.3.slab_back_ref
  24.4 0.0 collective-permute-done.2.brick_back_ref
  24.4 0.0 collective-permute-done.1.slab_next_ref
  24.4 0.0 collective-permute-done.brick_next_ref
  24.4 0.0 copy-done.5
  24.4 4.5 %outer.1 = (f32[77,256]{1,0:T(8,128)}, f32[128,128]{1,0:T(8,128)S(1)}) custom-call(f32[72,256]{1,0:T(8,128)S(1)} %pack.1.packed_ref, f32[72,256]{1,0:T(8,128)S(1)} %collective-permute-done.brick_next_ref, f32[72,256]{1,0:T(8,128)S(1)} %collective-permute-done.1.slab_next_ref, f32[72,256]{1,0:T(8,128)S(1)} %collective-permute-done.2.brick_back_ref, ...), custom_call_target="tpu_custom_call" | custom-call | flops 30000000 | bytes 400000 | tf_op jit(solution)/shard_map/outer/pallas_call | solution.py:351
  28.9 19.8 %all_to_all.5 = f32[64,2,128]{2,1,0:T(2,128)S(1)} all-to-all(f32[64,2,128]{2,1,0:T(2,128)S(1)} %bitcast.9), channel_id=1, replica_groups=mesh['slab'=8,'brick'=64] {'brick'}, dimensions={0} | all-to-all | bytes 131072 | tf_op jit(solution)/shard_map/all_to_all | solution.py:378
  48.7 0.7 %turn.1 = f32[77,128]{1,0:T(8,128)} custom-call(f32[128,128]{1,0:T(8,128)S(1)} %bitcast.8), custom_call_target="tpu_custom_call" | custom-call | tf_op jit(solution)/shard_map/turn/pallas_call | solution.py:379
Async XLA Ops:
  0.6 0.7 %copy-start.1 = (f32[3,256]{1,0:T(4,128)S(1)}, f32[3,256]{1,0:T(4,128)}, u32[]{:S(2)}) copy-start(f32[3,256]{1,0:T(4,128)} %pos_ref.1) | copy-start | bytes 9220
  1.3 0.7 %copy-start.3 = (s32[64]{0:T(128)S(1)}, s32[64]{0:T(128)}, u32[]{:S(2)}) copy-start(s32[64]{0:T(128)} %param.17) | copy-start | bytes 772
  1.3 0.7 %copy-start.4 = (s32[64]{0:T(128)S(1)}, s32[64]{0:T(128)}, u32[]{:S(2)}) copy-start(s32[64]{0:T(128)} %param.18) | copy-start | bytes 772
  2.0 0.8 %copy-start = (f32[64,256]{1,0:T(8,128)S(1)}, f32[64,256]{1,0:T(8,128)}, u32[]{:S(2)}) copy-start(f32[64,256]{1,0:T(8,128)} %hist_ref.1) | copy-start | bytes 196612
  2.8 0.7 %copy-start.2 = (f32[4,256]{1,0:T(4,128)S(1)}, f32[4,256]{1,0:T(4,128)}, u32[]{:S(2)}) copy-start(f32[4,256]{1,0:T(4,128)} %ori_ref.1) | copy-start | bytes 12292
  3.6 20.8 %collective-permute-start.3 = (f32[72,256]{1,0:T(8,128)S(1)}, f32[72,256]{1,0:T(8,128)S(1)}, u32[]{:S(2)}, u32[]{:S(2)}) collective-permute-start(f32[72,256]{1,0:T(8,128)S(1)} %pack.1.packed_ref), channel_id=1, source_target_pairs={{0,64},{64,128},{128,192},{192,256},{256,320},{320,384},{384,448},... | collective-permute-start | bytes 221192 | tf_op jit(solution)/shard_map/ppermute | solution.py:299
  3.6 20.8 %collective-permute-start.2 = (f32[72,256]{1,0:T(8,128)S(1)}, f32[72,256]{1,0:T(8,128)S(1)}, u32[]{:S(2)}, u32[]{:S(2)}) collective-permute-start(f32[72,256]{1,0:T(8,128)S(1)} %pack.1.packed_ref), channel_id=1, source_target_pairs={{0,1},{1,2},{2,3},{3,4},{4,5},{5,6},{6,7},{7,8},{8,9},{9,10},{10,1... | collective-permute-start | bytes 221192 | tf_op jit(solution)/shard_map/ppermute | solution.py:299
  7.9 16.6 %collective-permute-start.1 = (f32[72,256]{1,0:T(8,128)S(1)}, f32[72,256]{1,0:T(8,128)S(1)}, u32[]{:S(2)}, u32[]{:S(2)}) collective-permute-start(f32[72,256]{1,0:T(8,128)S(1)} %pack.1.packed_ref), channel_id=1, source_target_pairs={{0,448},{64,0},{128,64},{192,128},{256,192},{320,256},{384,320},{4... | collective-permute-start | bytes 221192 | tf_op jit(solution)/shard_map/ppermute | solution.py:299
  9.3 15.1 %collective-permute-start = (f32[72,256]{1,0:T(8,128)S(1)}, f32[72,256]{1,0:T(8,128)S(1)}, u32[]{:S(2)}, u32[]{:S(2)}) collective-permute-start(f32[72,256]{1,0:T(8,128)S(1)} %pack.1.packed_ref), channel_id=1, source_target_pairs={{0,63},{1,0},{2,1},{3,2},{4,3},{5,4},{6,5},{7,6},{8,7},{9,8},{10,9... | collective-permute-start | bytes 221192 | tf_op jit(solution)/shard_map/ppermute | solution.py:299
  21.1 0.7 %copy-start.10 = (s32[64,1]{0,1:T(1,128)S(1)}, s32[64,1]{0,1:T(1,128)}, u32[]{:S(2)}) copy-start(s32[64,1]{0,1:T(1,128)} %param.23) | copy-start | bytes 772
  21.1 0.7 %copy-start.6 = (f32[3,64]{1,0:T(4,128)S(1)}, f32[3,64]{1,0:T(4,128)}, u32[]{:S(2)}) copy-start(f32[3,64]{1,0:T(4,128)} %template_ref.3) | copy-start | bytes 2308
  21.1 0.7 %copy-start.7 = (s32[64]{0:T(128)S(1)}, s32[64]{0:T(128)}, u32[]{:S(2)}) copy-start(s32[64]{0:T(128)} %param.20) | copy-start | bytes 772
  21.1 0.7 %copy-start.8 = (s32[64]{0:T(128)S(1)}, s32[64]{0:T(128)}, u32[]{:S(2)}) copy-start(s32[64]{0:T(128)} %param.21) | copy-start | bytes 772
  21.1 0.7 %copy-start.9 = (s32[64]{0:T(128)S(1)}, s32[64]{0:T(128)}, u32[]{:S(2)}) copy-start(s32[64]{0:T(128)} %param.22) | copy-start | bytes 772
  21.8 2.6 %copy-start.5 = (f32[6,256]{1,0:T(8,128)S(1)}, f32[6,256]{1,0:T(8,128)}, u32[]{:S(2)}) copy-start(f32[6,256]{1,0:T(8,128)} %velocity_ref.1) | copy-start | bytes 18436

commit v3 on v2

v3 whole, which is shorter than its diff:
```python
import jax
import jax.numpy as jnp
from jax import lax
from jax.experimental import pallas as pl
from jax.experimental.pallas import tpu as pltpu
from jax.sharding import PartitionSpec as P

MEMBERS = 64
CLUMPS = 256
LANES = 128
PAIRS = 64
HALF = MEMBERS // 2
SLOT_CAP = 2
BRICKS = 64
CHUNK = 2 * SLOT_CAP
VMEM_LIMIT = 8 * 1024 * 1024
IDLE = 1024

DIAMETER = 0.3
SOFTENING = 0.0001
TIME_STEP = 0.02
INERTIA_SCALE = 0.05
HISTORY_DECAY = 0.9

POS = MEMBERS
ORI = MEMBERS + 3
LISTS = MEMBERS + 7
PACKED = MEMBERS + 8

F32 = jnp.float32
BF16 = jnp.bfloat16
I32 = jnp.int32


def parts_of(value):
    high = value.astype(BF16)
    rest = value - high.astype(F32)
    middle = rest.astype(BF16)
    low = (rest - middle.astype(F32)).astype(BF16)
    return (high, middle, low)


def one_hot(index_row, rows=CLUMPS):
    count = lax.broadcasted_iota(I32, (rows, index_row.shape[1]), 0)
    return jnp.where(count == index_row, 1.0, 0.0).astype(F32).astype(BF16)


def gather(parts, chosen):
    high, middle, low = [jnp.dot(part, chosen, preferred_element_type=F32) for part in parts]
    return high + middle + low


def scatter(value, chosen):
    dims = (((1,), (1,)), ((), ()))
    high, middle, low = [
        lax.dot_general(part, chosen, dims, preferred_element_type=F32) for part in parts_of(value)
    ]
    return high + middle + low


def arms_of(picked, template):
    quat = [picked[ORI + k : ORI + k + 1] for k in range(4)]
    scale = lax.rsqrt(quat[0] * quat[0] + quat[1] * quat[1] + quat[2] * quat[2] + quat[3] * quat[3])
    qw, qx, qy, qz = [q * scale for q in quat]
    matrix = [
        [1.0 - 2.0 * (qy * qy + qz * qz), 2.0 * (qx * qy - qw * qz), 2.0 * (qx * qz + qw * qy)],
        [2.0 * (qx * qy + qw * qz), 1.0 - 2.0 * (qx * qx + qz * qz), 2.0 * (qy * qz - qw * qx)],
        [2.0 * (qx * qz - qw * qy), 2.0 * (qy * qz + qw * qx), 1.0 - 2.0 * (qx * qx + qy * qy)],
    ]
    return [row[0] * template[0] + row[1] * template[1] + row[2] * template[2] for row in matrix]


def spread_template(template_ref):
    padded = jnp.concatenate([template_ref[...], jnp.zeros((5, MEMBERS), F32)], 0)
    turned = padded.T
    return [jnp.broadcast_to(turned[:, k : k + 1], (MEMBERS, LANES)) for k in range(3)]


def twice(row):
    return jnp.concatenate([row, row], 1)


def halves(value):
    lane = lax.broadcasted_iota(I32, (HALF, LANES), 1)
    return jnp.where(lane < PAIRS, value[:HALF], value[HALF:])


def place_source(src_ref, picked, arm, shift):
    for k in range(3):
        src_ref[k] = (picked[POS + k : POS + k + 1] + shift[k]) + arm[k]
    src_ref[3] = 10.0 + 10.0 * picked[0:MEMBERS]


def contact(place, weight, src_ref):
    def step(b, sums):
        other = [src_ref[k, pl.ds(b, 1), :] for k in range(4)]
        dx = place[0] - other[0]
        dy = place[1] - other[1]
        dz = place[2] - other[2]
        square = dx * dx + dy * dy + (dz * dz + SOFTENING)
        inverse = lax.rsqrt(square)
        margin = jnp.maximum(DIAMETER - square * inverse, 0.0)
        push = margin * inverse * (weight + other[3])
        return (sums[0] + push * dx, sums[1] + push * dy, sums[2] + push * dz, sums[3] + margin)

    zero = jnp.zeros((HALF, LANES), F32)
    return lax.fori_loop(0, MEMBERS, step, (zero, zero, zero, zero), unroll=4)


def body_rows(arm, force):
    turn = [
        arm[1] * force[2] - arm[2] * force[1],
        arm[2] * force[0] - arm[0] * force[2],
        arm[0] * force[1] - arm[1] * force[0],
    ]
    return jnp.concatenate(
        [jnp.sum(v, axis=0, keepdims=True) for v in list(force) + turn]
        + [jnp.zeros((2, LANES), F32)],
        0,
    )


def full_batch(picked, template, src_ref):
    arm = arms_of(picked, template)
    weight = 10.0 + 10.0 * picked[0:MEMBERS]
    tail = jnp.zeros((8, LANES), F32)
    margins = []
    for cut in (slice(0, HALF), slice(HALF, MEMBERS)):
        own = [a[cut] for a in arm]
        place = [picked[POS + k : POS + k + 1] + own[k] for k in range(3)]
        out = contact(place, weight[cut], src_ref)
        margins.append(out[3])
        tail = tail + body_rows(own, out[0:3])
    return jnp.concatenate(margins + [tail], 0)


def half_targets(picked, template):
    arm = arms_of(picked, [halves(t) for t in template])
    weight = 10.0 + 10.0 * halves(picked[0:MEMBERS])
    place = [picked[POS + k : POS + k + 1] + arm[k] for k in range(3)]
    return place, weight, arm


def half_rows(arm, out):
    lane = lax.broadcasted_iota(I32, (HALF, LANES), 1)
    lower = jnp.where(lane < PAIRS, out[3], 0.0)
    upper = jnp.where(lane < PAIRS, 0.0, out[3])
    return jnp.concatenate([lower, upper, body_rows(arm, out[0:3])], 0)


def contact_both(place, weight, src_ref, acc_ref):
    def step(b, sums):
        other = [src_ref[k, pl.ds(b, 1), :] for k in range(4)]
        offset = [place[k] - other[k] for k in range(3)]
        square = offset[0] * offset[0] + offset[1] * offset[1] + (offset[2] * offset[2] + SOFTENING)
        inverse = lax.rsqrt(square)
        margin = jnp.maximum(DIAMETER - square * inverse, 0.0)
        push = margin * inverse * (weight + other[3])
        terms = [push * d for d in offset] + [margin]
        for k in range(4):
            acc_ref[k, pl.ds(pl.multiple_of(b * 8, 8), 8), :] = jnp.sum(terms[k].reshape(HALF // 8, 8, LANES), axis=0)
        return tuple(total + term for total, term in zip(sums, terms))

    zero = jnp.zeros((HALF, LANES), F32)
    return lax.fori_loop(0, MEMBERS, step, (zero, zero, zero, zero), unroll=4)


def source_sums(acc_ref):
    out = []
    for k in range(4):
        rows = [acc_ref[k, pl.ds(r, MEMBERS, stride=8), :] for r in range(8)]
        out.append(((rows[0] + rows[1]) + (rows[2] + rows[3])) + ((rows[4] + rows[5]) + (rows[6] + rows[7])))
    return out


def routes(leaving, dest, first_row):
    to = one_hot(dest, BRICKS)
    before = lax.broadcasted_iota(I32, (PAIRS, PAIRS), 0) < lax.broadcasted_iota(I32, (PAIRS, PAIRS), 1)
    before = jnp.where(before, 1.0, 0.0).astype(BF16)
    earlier = jnp.dot(to, before, preferred_element_type=F32)
    rank = jnp.sum(earlier * to.astype(F32), axis=0, keepdims=True).astype(I32)
    return one_hot(dest * CHUNK + first_row + rank, BRICKS * CHUNK), one_hot(leaving)


def spin(angular, orient):
    wx, wy, wz = [angular[k : k + 1] for k in range(3)]
    ow, ox, oy, oz = orient
    return [
        -(wx * ox + wy * oy + wz * oz),
        ow * wx + (wy * oz - wz * oy),
        ow * wy + (wz * ox - wx * oz),
        ow * wz + (wx * oy - wy * ox),
    ]


def change_of(totals, orient):
    linear = TIME_STEP * totals[MEMBERS : MEMBERS + 3]
    angular = TIME_STEP * totals[MEMBERS + 3 : MEMBERS + 6] / INERTIA_SCALE
    turned = [0.5 * TIME_STEP * part for part in spin(angular, orient)]
    return jnp.concatenate([TIME_STEP * linear] + turned + [linear, angular], 0), totals[0:MEMBERS]


def orient_of(packed):
    return [packed[ORI + k : ORI + k + 1] for k in range(4)]


def to_slots(route, rows):
    dims = (((1,), (1,)), ((), ()))
    high, middle, low = [
        lax.dot_general(route, part, dims, preferred_element_type=F32) for part in parts_of(rows)
    ]
    return high + middle + low


def padded(head, history):
    return jnp.concatenate([history, head, jnp.zeros((LANES - 77, head.shape[1]), F32)], 0)


def pack_kernel(
    pos_hbm,
    ori_hbm,
    hist_hbm,
    velocity_hbm,
    template_hbm,
    local_hbm,
    ghost_hbm,
    first_hbm,
    gap_hbm,
    leaving_hbm,
    dest_hbm,
    count_ref,
    packed_ref,
    velocity_ref,
    template_ref,
    local_ref,
    ghost_ref,
    first_ref,
    gap_ref,
    leaving_ref,
    dest_ref,
    pos_ref,
    ori_ref,
    sems,
):
    moves = [
        (hist_hbm, packed_ref.at[0:MEMBERS]),
        (pos_hbm, pos_ref),
        (ori_hbm, ori_ref),
        (local_hbm, local_ref),
        (ghost_hbm, ghost_ref),
        (leaving_hbm, leaving_ref),
        (dest_hbm, dest_ref),
        (velocity_hbm, velocity_ref),
        (template_hbm, template_ref),
        (first_hbm, first_ref),
        (gap_hbm, gap_ref),
    ]
    copies = [pltpu.make_async_copy(a, b, sems.at[k]) for k, (a, b) in enumerate(moves)]
    for copy in copies:
        copy.start()
    for copy in copies[1:]:
        copy.wait()
    live = lax.broadcasted_iota(I32, (1, PAIRS), 1) < count_ref[0]
    ghost = ghost_ref[...]
    code = jnp.where(live, ghost, ghost + IDLE)
    lists = jnp.concatenate([local_ref[...], code, leaving_ref[...], dest_ref[...]], 1).astype(F32)
    packed_ref[MEMBERS:PACKED] = jnp.concatenate([pos_ref[...], ori_ref[...], lists], 0)
    copies[0].wait()


def inner_kernel(
    packed_ref,
    template_ref,
    first_ref,
    gap_ref,
    leaving_ref,
    dest_ref,
    local_ref,
    totals_ref,
    route_ref,
    departed_ref,
    spread_ref,
    target_ref,
    src_ref,
):
    template = spread_template(template_ref)
    for k in range(3):
        spread_ref[k] = template[k]
    column, leaves = routes(leaving_ref[...], dest_ref[...], 0)
    dims = (((1,), (1,)), ((), ()))
    route_ref[...] = lax.dot_general(column, leaves, dims, preferred_element_type=F32)
    ones = jnp.ones((8, PAIRS), F32).astype(BF16)
    departed_ref[...] = lax.dot_general(ones, leaves, dims, preferred_element_type=F32)

    own = parts_of(packed_ref[...])
    place, weight, arm = half_targets(gather(own, one_hot(twice(local_ref[...]))), template)
    for k in range(3):
        target_ref[k] = place[k]
        target_ref[4 + k] = arm[k]
    target_ref[3] = weight

    first = first_ref[...]
    second = jnp.bitwise_and(first + gap_ref[...], CLUMPS - 1)
    target = one_hot(jnp.concatenate([first, second], 1))
    source = one_hot(jnp.concatenate([second, first], 1))
    picked = gather(own, source)
    place_source(src_ref, picked, arms_of(picked, template), (0.0, 0.0, 0.0))
    rows = full_batch(gather(own, target), template, src_ref)
    totals_ref[...] = scatter(rows, target)


def slab_kernel(packed_ref, back_ref, next_ref, inner_ref, spread_ref, ghost_ref, totals_ref, picked_ref, src_ref):
    template = [spread_ref[k] for k in range(3)]
    lists = back_ref[LISTS : LISTS + 1].astype(I32)
    local, code = twice(lists[:, 0:PAIRS]), twice(lists[:, PAIRS : 2 * PAIRS])
    picked_ref[...] = gather(parts_of(next_ref[...]), one_hot(twice(ghost_ref[...]) - CLUMPS))
    source = gather(parts_of(back_ref[...]), one_hot(local))
    place_source(src_ref, source, arms_of(source, template), (-1.0, 0.0, 0.0))
    chosen = one_hot(jnp.bitwise_and(code, CLUMPS - 1))
    place, weight, arm = half_targets(gather(parts_of(packed_ref[...]), chosen), template)
    rows = half_rows(arm, contact(place, weight, src_ref))
    totals_ref[...] = inner_ref[...] + scatter(rows, one_hot(code - CLUMPS))


def brick_kernel(
    packed_ref,
    next_ref,
    picked_ref,
    totals_ref,
    velocity_ref,
    spread_ref,
    target_ref,
    local_ref,
    ghost_ref,
    count_ref,
    route_ref,
    state_ref,
    back_ref,
    buffer_ref,
    src_ref,
    acc_ref,
):
    template = [spread_ref[k] for k in range(3)]
    live = lax.broadcasted_iota(I32, (1, PAIRS), 1) < count_ref[0]
    local = twice(jnp.where(live, local_ref[...], IDLE))
    ghost = twice(ghost_ref[...])
    near = ghost < CLUMPS
    near_live = twice(jnp.where(live, ghost_ref[...], IDLE))

    picked = picked_ref[...] + gather(parts_of(next_ref[...]), one_hot(ghost))
    shift = (jnp.where(near, 0.0, 1.0), jnp.where(near, 1.0, 0.0), 0.0)
    arm_b = arms_of(picked, template)
    place_source(src_ref, picked, arm_b, shift)
    lists = next_ref[LISTS : LISTS + 1].astype(I32)
    column, leaves = routes(lists[:, 2 * PAIRS : 3 * PAIRS], lists[:, 3 * PAIRS :], SLOT_CAP)
    ghosts = one_hot(near_live)
    moving = lax.dot_general(leaves, ghosts, (((0,), (0,)), ((), ())), preferred_element_type=F32)
    moving = jnp.dot(column, moving.astype(BF16), preferred_element_type=F32).astype(BF16)

    out = contact_both([target_ref[k] for k in range(3)], target_ref[3], src_ref, acc_ref)
    rows = half_rows([target_ref[4 + k] for k in range(3)], out)
    totals = totals_ref[...] + scatter(rows, one_hot(local))
    force_x, force_y, force_z, margin = source_sums(acc_ref)
    rows = jnp.concatenate([margin, -body_rows(arm_b, (force_x, force_y, force_z))], 0)
    back_ref[...] = scatter(rows, ghosts)

    state = packed_ref[...]
    head, history = change_of(totals, orient_of(state))
    velocity = velocity_ref[...]
    start = jnp.concatenate([state[POS : POS + 3] + TIME_STEP * velocity[0:3], state[ORI : ORI + 4], velocity], 0)
    drift = [0.5 * TIME_STEP * part for part in spin(velocity[3:6], orient_of(state))]
    nothing = jnp.zeros((3, CLUMPS), F32)
    head = head + start + jnp.concatenate([nothing] + drift + [nothing, nothing], 0)
    full = padded(head, HISTORY_DECAY * state[0:MEMBERS] + history)
    state_ref[...] = full
    head, history = change_of(rows, orient_of(picked))
    buffer_ref[...] = to_slots(route_ref[...].astype(BF16), full) + to_slots(moving, padded(head, history))


def stay_kernel(state_ref, packed_ref, back_ref, departed_ref, staying_ref):
    departed = departed_ref[0:1] > 0.5
    head, history = change_of(back_ref[...], orient_of(packed_ref[...]))
    staying_ref[0:13] = jnp.where(departed, 0.0, state_ref[MEMBERS : MEMBERS + 13] + head)
    staying_ref[13:77] = jnp.where(departed, 0.0, state_ref[0:MEMBERS] + history)


def turn_kernel(in_ref, out_ref, row_ref):
    for slot in range(SLOT_CAP):
        own = in_ref[pl.ds(slot, BRICKS, stride=CHUNK), :]
        more = in_ref[pl.ds(SLOT_CAP + slot, BRICKS, stride=CHUNK), :]
        more = jnp.concatenate([more[BRICKS - 1 :], more[: BRICKS - 1]], 0)
        row_ref[pl.ds(slot, BRICKS, stride=SLOT_CAP), :] = own + more
    turned = row_ref[...].T
    out_ref[0:13] = turned[MEMBERS : MEMBERS + 13]
    out_ref[13:77] = turned[0:MEMBERS]


def vmem():
    return pl.BlockSpec(memory_space=pltpu.VMEM)


def smem():
    return pl.BlockSpec(memory_space=pltpu.SMEM)


def hbm():
    return pl.BlockSpec(memory_space=pltpu.HBM)


def small():
    return pltpu.CompilerParams(vmem_limit_bytes=VMEM_LIMIT)


def cost(flops):
    return pl.CostEstimate(flops=flops, bytes_accessed=400_000, transcendentals=flops // 30)


def array(*shape, dtype=F32):
    return jax.ShapeDtypeStruct(shape, dtype)


def from_behind(value, axis, steps):
    count = lax.axis_size(axis)
    pairs = [(source, (source + steps) % count) for source in range(count)]
    return lax.ppermute(value, axis, pairs)


def shards(
    position,
    orient,
    velocity,
    history,
    template,
    cross_local,
    cross_ghost,
    cross_count,
    inner_first,
    inner_gap,
    mig_index,
    mig_dest,
):
    lists = [v.reshape(1, PAIRS) for v in (cross_local, cross_ghost, inner_first, inner_gap, mig_index, mig_dest)]
    loads = [
        pltpu.with_memory_space_constraint(v, pltpu.HBM)
        for v in (position, orient, history, velocity, template, *lists)
    ]
    packed, velocity, template, local, ghost, first, gap, leaving, dest = pl.pallas_call(
        pack_kernel,
        out_shape=(array(PACKED, CLUMPS), array(6, CLUMPS), array(3, MEMBERS)) + (array(1, PAIRS, dtype=I32),) * 6,
        in_specs=[hbm()] * 11 + [smem()],
        out_specs=(vmem(),) * 9,
        scratch_shapes=[
            pltpu.VMEM((3, CLUMPS), F32),
            pltpu.VMEM((4, CLUMPS), F32),
            pltpu.SemaphoreType.DMA((11,)),
        ],
        compiler_params=small(),
        name="pack",
    )(*loads, cross_count)
    slab_next = from_behind(packed, "slab", -1)
    slab_back = from_behind(packed, "slab", 1)
    brick_next = from_behind(packed, "brick", -1)
    totals, route, departed, spread, target = pl.pallas_call(
        inner_kernel,
        out_shape=(
            array(PACKED, CLUMPS),
            array(BRICKS * CHUNK, CLUMPS),
            array(8, CLUMPS),
            array(3, MEMBERS, LANES),
            array(7, HALF, LANES),
        ),
        in_specs=[vmem()] * 7,
        out_specs=(vmem(),) * 5,
        scratch_shapes=[pltpu.VMEM((4, MEMBERS, LANES), F32)],
        cost_estimate=cost(20_000_000),
        compiler_params=small(),
        name="inner",
    )(packed, template, first, gap, leaving, dest, local)
    totals, picked = pl.pallas_call(
        slab_kernel,
        out_shape=(array(PACKED, CLUMPS), array(PACKED, LANES)),
        in_specs=[vmem()] * 6,
        out_specs=(vmem(),) * 2,
        scratch_shapes=[pltpu.VMEM((4, MEMBERS, LANES), F32)],
        cost_estimate=cost(10_000_000),
        compiler_params=small(),
        name="slab",
    )(packed, slab_back, slab_next, totals, spread, ghost)
    state, back, buffer = pl.pallas_call(
        brick_kernel,
        out_shape=(array(LANES, CLUMPS), array(PACKED, CLUMPS), array(BRICKS * CHUNK, LANES)),
        in_specs=[vmem()] * 9 + [smem(), vmem()],
        out_specs=(vmem(),) * 3,
        scratch_shapes=[
            pltpu.VMEM((4, MEMBERS, LANES), F32),
            pltpu.VMEM((4, 8 * MEMBERS, LANES), F32),
        ],
        cost_estimate=cost(15_000_000),
        compiler_params=small(),
        name="brick",
    )(packed, brick_next, picked, totals, velocity, spread, target, local, ghost, cross_count, route)
    arrived = lax.all_to_all(buffer.reshape(BRICKS, CHUNK, LANES), "brick", split_axis=0, concat_axis=0)
    back = from_behind(back, "brick", 1)
    staying = pl.pallas_call(
        stay_kernel,
        out_shape=array(77, CLUMPS),
        in_specs=[vmem()] * 4,
        out_specs=vmem(),
        cost_estimate=cost(5_000_000),
        compiler_params=small(),
        name="stay",
    )(state, packed, back, departed)
    arrivals = pl.pallas_call(
        turn_kernel,
        out_shape=array(77, BRICKS * SLOT_CAP),
        in_specs=[vmem()],
        out_specs=vmem(),
        scratch_shapes=[pltpu.VMEM((BRICKS * SLOT_CAP, LANES), F32)],
        compiler_params=small(),
        name="turn",
    )(arrived.reshape(BRICKS * CHUNK, LANES))
    return (staying, arrivals)


def solution(mesh):
    both = ("slab", "brick")
    return jax.shard_map(
        shards,
        mesh=mesh,
        in_specs=(
            P(None, both),
            P(None, both),
            P(None, both),
            P(None, both),
            P(),
            P(both),
            P(both),
            P(both),
            P(both),
            P(both),
            P(both),
            P(both, None),
        ),
        out_specs=(P(None, both), P(None, both)),
        check_vma=False,
    )
```

time: 50 us -> 45.1 us (0.902)
  blocking collectives: 19.8 us -> 0 us
  waiting for transfers between devices: 0.01 us -> 9.47 us
  starting transfers between devices: 17.5 us -> 24.7 us
  local copies, waits for them, and re-layouts: 2.86 us -> 0 us
  Pallas kernels: 7.85 us -> 9.32 us
    all_to_all x1 -> x0, blocking collectives: 19.8 us -> none  [shards(): lax.all_to_all(buffer.reshape(64, SLOT_CAP, LANES), 'brick', split_axis=0...]
    ppermute x4, waiting for transfers between devices: 0.01 us -> 7.66 us  [from_behind(): return lax.ppermute(value, axis, pairs)]
    all_to_all x0 -> x1, starting transfers between devices: none -> 6.86 us  [shards(): lax.all_to_all(buffer.reshape(BRICKS, CHUNK, LANES), 'brick', split_axis=...]
    unnamed x22 -> x0, local copies, waits for them, and re-layouts: 2.86 us -> none
    all_to_all x0 -> x1, waiting for transfers between devices: none -> 1.81 us  [shards(): lax.all_to_all(buffer.reshape(BRICKS, CHUNK, LANES), 'brick', split_axis=...]
    pallas_call x4 -> x6, Pallas kernels: 7.85 us -> 9.32 us  [the longest x1 2.76 us: shards(): pl.pallas_call(brick_kernel, out_shape=(array(LANES, CLUMPS), array(PACKE...]
  transfers between devices with their start and end apart: 4 -> 5, of which waited for: 0 -> 2; matrix products, arithmetic and copies ran while one was open for 0% -> 0% of each run, Pallas kernels for 5% -> 11%
where the time goes in v3:
time: 45.1 us; the launch traced here: 44.8 us
  starting transfers between devices  24.7 us (55%)
  waiting for transfers between devices  9.47 us (21%)
  Pallas kernels  9.32 us (21%)
  between operations  1.35 us (3%)
    ppermute x4, starting transfers between devices, from_behind(): return lax.ppermute(value, axis, pairs)  17.8 us
    ppermute x4, waiting for transfers between devices, from_behind(): return lax.ppermute(value, axis, pairs)  7.66 us
    all_to_all x1, starting transfers between devices, shards(): lax.all_to_all(buffer.reshape(BRICKS, CHUNK, LANES), 'brick', split_axis=...  6.86 us
    pallas_call x1, Pallas kernels, shards(): pl.pallas_call(brick_kernel, out_shape=(array(LANES, CLUMPS), array(PACKE...  2.76 us
    pallas_call x1, Pallas kernels, shards(): pl.pallas_call(inner_kernel, out_shape=(array(PACKED, CLUMPS), array(BRIC...  2.64 us
    all_to_all x1, waiting for transfers between devices, shards(): lax.all_to_all(buffer.reshape(BRICKS, CHUNK, LANES), 'brick', split_axis=...  1.81 us
    pallas_call x1, Pallas kernels, shards(): pl.pallas_call(slab_kernel, out_shape=(array(PACKED, CLUMPS), array(PACKE...  1.53 us
    pallas_call x1, Pallas kernels, shards(): pl.pallas_call(pack_kernel, out_shape=(array(PACKED, CLUMPS), array(6, CL...  1.01 us
  transfers between devices with their start and end apart: 5, of which 2 were waited for; matrix products, arithmetic and copies ran while one was open for 0% of the time, Pallas kernels for 11%

profile of v3, /device:TPU:6, one launch (start us, length us, event | category | flops | bytes accessed | tf_op | source)
XLA Modules:
  0.0 44.8 jit_solution(2505784149185607638)
XLA Ops:
  1.3 1.0 %pack.1 = (f32[72,256]{1,0:T(8,128)S(1)}, f32[6,256]{1,0:T(8,128)S(1)}, f32[3,64]{1,0:T(4,128)S(1)}, s32[1,64]{1,0:T(1,128)S(1)}, s32[1,64]{1,0:T(1,128)S(1)}, /...) custom-call(f32[3,256]{1,0:T(4,128)} %pos_hbm.1, f32[4,256]{1,0:T(4,128)} %ori_hbm.1, ...), custom_call_target="tpu_custom_call" | custom-call | tf_op jit(solution)/shard_map/pack/pallas_call | solution.py:447
  2.3 0.3 collective-permute-start.2
  2.6 0.2 collective-permute-start.1
  2.8 13.8 %collective-permute-start = (f32[72,256]{1,0:T(8,128)S(1)}, f32[72,256]{1,0:T(8,128)S(1)}, u32[]{:S(2)}, u32[]{:S(2)}) collective-permute-start(f32[72,256]{1,0:T(8,128)S(1)} %get-tuple-element.21.packed_ref), channel_id=1, source_target_pairs={{0,63},{1,0},{2,1},{3,2},{4,3},{5,4},{6,5},{7,6},{8,7},{9,8},{10,9... | collective-permute-start | bytes 221192 | tf_op jit(solution)/shard_map/ppermute | solution.py:425
  16.7 2.6 %inner.1 = (f32[72,256]{1,0:T(8,128)S(1)}, f32[256,256]{1,0:T(8,128)S(1)}, f32[8,256]{1,0:T(8,128)S(1)}, f32[3,64,128]{2,1,0:T(8,128)S(1)}, f32[7,32,128]{2,1,0:T(8,128)S(1)}) custom-call(f32[72,256]{1,0:T(8,128)S(1)} %get-tuple-element.21.packed_ref, f32[3,64]{1,0:T(4,128)S(1)} %get-tuple-element.22.template_ref, s32[1,64]{1,0:T(1,128)S(1)} %get-tuple-element.23.first_ref, ...), custom_call_target="tpu_custom_call" | custom-call | flops 20000000 | bytes 400000 | tf_op jit(solution)/shard_map/inner/pallas_call | solution.py:463
  19.3 0.0 collective-permute-done.2.next_ref
  19.3 0.0 collective-permute-done.1.back_ref
  19.3 1.5 %slab.1 = (f32[72,256]{1,0:T(8,128)S(1)}, f32[72,128]{1,0:T(8,128)S(1)}) custom-call(f32[72,256]{1,0:T(8,128)S(1)} %get-tuple-element.21.packed_ref, f32[72,256]{1,0:T(8,128)S(1)} %collective-permute-done.1.back_ref, f32[72,256]{1,0:T(8,128)S(1)} %collective-permute-done.2.next_ref, f32[72,256]{1,0:T(8,128)S(1)} %get-tuple-element.28.inner_ref, ...), custom_call_target="tpu_custom_call" | custom-call | flops 10000000 | bytes 400000 | tf_op jit(solution)/shard_map/slab/pallas_call | solution.py:479
  20.9 0.0 collective-permute-done.next_ref
  20.9 2.8 %brick.1 = (f32[128,256]{1,0:T(8,128)S(1)}, f32[72,256]{1,0:T(8,128)S(1)}, f32[256,128]{1,0:T(8,128)}) custom-call(f32[72,256]{1,0:T(8,128)S(1)} %get-tuple-element.21.packed_ref, f32[72,256]{1,0:T(8,128)S(1)} %collective-permute-done.next_ref, f32[72,128]{1,0:T(8,128)S(1)} %get-tuple-element.31.picked_ref, f32[72,256]{1,0:T(8,128)S(1)} %get-tuple-element.32.totals_ref, ...), custom_call_target="tpu_custom_call" | custom-call | flops 15000000 | bytes 400000 | tf_op jit(solution)/shard_map/brick/pallas_call | solution.py:489
  23.6 6.9 %all-to-all-start = ((f32[64,4,128]{2,1,0:T(4,128)}), f32[64,4,128]{2,1,0:T(4,128)S(1)}, u32[]{:S(2)}, u32[]{:S(2)}) async-start(f32[64,4,128]{2,1,0:T(4,128)} %bitcast.6), calls=%async_computation | async-start | bytes 262144 | tf_op jit(solution)/shard_map/all_to_all | solution.py:502
  30.5 3.5 %collective-permute-start.3 = (f32[72,256]{1,0:T(8,128)S(1)}, f32[72,256]{1,0:T(8,128)S(1)}, u32[]{:S(2)}, u32[]{:S(2)}) collective-permute-start(f32[72,256]{1,0:T(8,128)S(1)} %get-tuple-element.37), channel_id=1, source_target_pairs={{0,1},{1,2},{2,3},{3,4},{4,5},{5,6},{6,7},{7,8},{8,9},{9,10},{10,1... | collective-permute-start | bytes 221192 | tf_op jit(solution)/shard_map/ppermute | solution.py:425
  34.0 7.7 %collective-permute-done.3.back_ref = f32[72,256]{1,0:T(8,128)S(1)} collective-permute-done((f32[72,256]{1,0:T(8,128)S(1)}, f32[72,256]{1,0:T(8,128)S(1)}, u32[]{:S(2)}, u32[]{:S(2)}) %collective-permute-start.3) | collective-permute-done | bytes 73760 | tf_op jit(solution)/shard_map/ppermute | solution.py:425
  41.7 0.7 %stay.1 = f32[77,256]{1,0:T(8,128)} custom-call(f32[128,256]{1,0:T(8,128)S(1)} %get-tuple-element.36.state_ref, f32[72,256]{1,0:T(8,128)S(1)} %get-tuple-element.21.packed_ref, f32[72,256]{1,0:T(8,128)S(1)} %collective-permute-done.3.back_ref, f32[8,256]{1,0:T(8,128)S(1)} %get-tuple-element.38.departed_ref), custom_call_target="tpu_custom_call" | custom-call | flops 5000000 | bytes 400000 | tf_op jit(solution)/shard_map/stay/pallas_call | solution.py:504
  42.3 1.8 %all-to-all-done = f32[64,4,128]{2,1,0:T(4,128)S(1)} async-done(((f32[64,4,128]{2,1,0:T(4,128)}), f32[64,4,128]{2,1,0:T(4,128)S(1)}, u32[]{:S(2)}, u32[]{:S(2)}) %all-to-all-start) | async-done | bytes 131104 | tf_op jit(solution)/shard_map/all_to_all | solution.py:502
  44.1 0.7 %turn.1 = f32[77,128]{1,0:T(8,128)} custom-call(f32[256,128]{1,0:T(8,128)S(1)} %bitcast.8), custom_call_target="tpu_custom_call" | custom-call | tf_op jit(solution)/shard_map/turn/pallas_call | solution.py:513
Async XLA Ops:
  2.3 17.0 %collective-permute-start.2 = (f32[72,256]{1,0:T(8,128)S(1)}, f32[72,256]{1,0:T(8,128)S(1)}, u32[]{:S(2)}, u32[]{:S(2)}) collective-permute-start(f32[72,256]{1,0:T(8,128)S(1)} %get-tuple-element.21.packed_ref), channel_id=1, source_target_pairs={{0,448},{64,0},{128,64},{192,128},{256,192},{320,256},{384,320},{4... | collective-permute-start | bytes 221192 | tf_op jit(solution)/shard_map/ppermute | solution.py:425
  2.6 16.7 %collective-permute-start.1 = (f32[72,256]{1,0:T(8,128)S(1)}, f32[72,256]{1,0:T(8,128)S(1)}, u32[]{:S(2)}, u32[]{:S(2)}) collective-permute-start(f32[72,256]{1,0:T(8,128)S(1)} %get-tuple-element.21.packed_ref), channel_id=1, source_target_pairs={{0,64},{64,128},{128,192},{192,256},{256,320},{320,384},{384,448},... | collective-permute-start | bytes 221192 | tf_op jit(solution)/shard_map/ppermute | solution.py:425
  2.8 18.1 %collective-permute-start = (f32[72,256]{1,0:T(8,128)S(1)}, f32[72,256]{1,0:T(8,128)S(1)}, u32[]{:S(2)}, u32[]{:S(2)}) collective-permute-start(f32[72,256]{1,0:T(8,128)S(1)} %get-tuple-element.21.packed_ref), channel_id=1, source_target_pairs={{0,63},{1,0},{2,1},{3,2},{4,3},{5,4},{6,5},{7,6},{8,7},{9,8},{10,9... | collective-permute-start | bytes 221192 | tf_op jit(solution)/shard_map/ppermute | solution.py:425
  23.6 20.5 %all-to-all-start = ((f32[64,4,128]{2,1,0:T(4,128)}), f32[64,4,128]{2,1,0:T(4,128)S(1)}, u32[]{:S(2)}, u32[]{:S(2)}) async-start(f32[64,4,128]{2,1,0:T(4,128)} %bitcast.6), calls=%async_computation | async-start | bytes 262144 | tf_op jit(solution)/shard_map/all_to_all | solution.py:502
  30.5 11.1 %collective-permute-start.3 = (f32[72,256]{1,0:T(8,128)S(1)}, f32[72,256]{1,0:T(8,128)S(1)}, u32[]{:S(2)}, u32[]{:S(2)}) collective-permute-start(f32[72,256]{1,0:T(8,128)S(1)} %get-tuple-element.37), channel_id=1, source_target_pairs={{0,1},{1,2},{2,3},{3,4},{4,5},{5,6},{6,7},{7,8},{8,9},{9,10},{10,1... | collective-permute-start | bytes 221192 | tf_op jit(solution)/shard_map/ppermute | solution.py:425

commit v4 on v3

v4 whole, which is shorter than its diff:
```python
import jax
import jax.numpy as jnp
from jax import lax
from jax.experimental import pallas as pl
from jax.experimental.pallas import tpu as pltpu
from jax.sharding import PartitionSpec as P

MEMBERS = 64
CLUMPS = 256
LANES = 128
PAIRS = 64
HALF = MEMBERS // 2
SLOT_CAP = 2
BRICKS = 64
FIRST = 36
ORDER = [FIRST ^ k for k in range(BRICKS)]
VMEM_LIMIT = 8 * 1024 * 1024
IDLE = 1024

DIAMETER = 0.3
SOFTENING = 0.0001
TIME_STEP = 0.02
INERTIA_SCALE = 0.05
HISTORY_DECAY = 0.9

POS = MEMBERS
ORI = MEMBERS + 3
LISTS = MEMBERS + 7
PACKED = MEMBERS + 8

LAST = (((1,), (1,)), ((), ()))
F32 = jnp.float32
BF16 = jnp.bfloat16
I32 = jnp.int32


def parts_of(value):
    high = value.astype(BF16).astype(F32)
    rest = value - high
    middle = rest.astype(BF16).astype(F32)
    return jnp.concatenate([high, middle, rest - middle], 0).astype(BF16)


def sum_parts(value):
    rows = value.shape[0] // 3
    return value[:rows] + value[rows : 2 * rows] + value[2 * rows :]


def one_hot(index_row, rows=CLUMPS):
    count = lax.broadcasted_iota(I32, (rows, index_row.shape[1]), 0)
    return jnp.where(count == index_row, 1.0, 0.0).astype(F32).astype(BF16)


def gather(parts, chosen):
    return sum_parts(jnp.dot(parts, chosen, preferred_element_type=F32))


def scatter(value, chosen):
    return sum_parts(lax.dot_general(parts_of(value), chosen, LAST, preferred_element_type=F32))


def arms_of(picked, template):
    quat = [picked[ORI + k : ORI + k + 1] for k in range(4)]
    scale = lax.rsqrt(quat[0] * quat[0] + quat[1] * quat[1] + quat[2] * quat[2] + quat[3] * quat[3])
    qw, qx, qy, qz = [q * scale for q in quat]
    matrix = [
        [1.0 - 2.0 * (qy * qy + qz * qz), 2.0 * (qx * qy - qw * qz), 2.0 * (qx * qz + qw * qy)],
        [2.0 * (qx * qy + qw * qz), 1.0 - 2.0 * (qx * qx + qz * qz), 2.0 * (qy * qz - qw * qx)],
        [2.0 * (qx * qz - qw * qy), 2.0 * (qy * qz + qw * qx), 1.0 - 2.0 * (qx * qx + qy * qy)],
    ]
    return [row[0] * template[0] + row[1] * template[1] + row[2] * template[2] for row in matrix]


def spread_template(template_ref):
    padded = jnp.concatenate([template_ref[...], jnp.zeros((5, MEMBERS), F32)], 0)
    turned = padded.T
    return [jnp.broadcast_to(turned[:, k : k + 1], (MEMBERS, LANES)) for k in range(3)]


def twice(row):
    return jnp.concatenate([row, row], 1)


def halves(value):
    lane = lax.broadcasted_iota(I32, (HALF, LANES), 1)
    return jnp.where(lane < PAIRS, value[:HALF], value[HALF:])


def place_source(src_ref, picked, arm, shift):
    for k in range(3):
        src_ref[k] = (picked[POS + k : POS + k + 1] + shift[k]) + arm[k]
    src_ref[3] = 10.0 + 10.0 * picked[0:MEMBERS]


def contact(place, weight, src_ref):
    def step(b, sums):
        other = [src_ref[k, pl.ds(b, 1), :] for k in range(4)]
        dx = place[0] - other[0]
        dy = place[1] - other[1]
        dz = place[2] - other[2]
        square = dx * dx + dy * dy + (dz * dz + SOFTENING)
        inverse = lax.rsqrt(square)
        margin = jnp.maximum(DIAMETER - square * inverse, 0.0)
        push = margin * inverse * (weight + other[3])
        return (sums[0] + push * dx, sums[1] + push * dy, sums[2] + push * dz, sums[3] + margin)

    zero = jnp.zeros((HALF, LANES), F32)
    return lax.fori_loop(0, MEMBERS, step, (zero, zero, zero, zero), unroll=4)


def body_rows(arm, force):
    turn = [
        arm[1] * force[2] - arm[2] * force[1],
        arm[2] * force[0] - arm[0] * force[2],
        arm[0] * force[1] - arm[1] * force[0],
    ]
    return jnp.concatenate(
        [jnp.sum(v, axis=0, keepdims=True) for v in list(force) + turn]
        + [jnp.zeros((2, LANES), F32)],
        0,
    )


def full_batch(picked, template, src_ref):
    arm = arms_of(picked, template)
    weight = 10.0 + 10.0 * picked[0:MEMBERS]
    tail = jnp.zeros((8, LANES), F32)
    margins = []
    for cut in (slice(0, HALF), slice(HALF, MEMBERS)):
        own = [a[cut] for a in arm]
        place = [picked[POS + k : POS + k + 1] + own[k] for k in range(3)]
        out = contact(place, weight[cut], src_ref)
        margins.append(out[3])
        tail = tail + body_rows(own, out[0:3])
    return jnp.concatenate(margins + [tail], 0)


def half_targets(picked, template):
    arm = arms_of(picked, [halves(t) for t in template])
    weight = 10.0 + 10.0 * halves(picked[0:MEMBERS])
    place = [picked[POS + k : POS + k + 1] + arm[k] for k in range(3)]
    return place, weight, arm


def half_rows(arm, out):
    lane = lax.broadcasted_iota(I32, (HALF, LANES), 1)
    lower = jnp.where(lane < PAIRS, out[3], 0.0)
    upper = jnp.where(lane < PAIRS, 0.0, out[3])
    return jnp.concatenate([lower, upper, body_rows(arm, out[0:3])], 0)


def contact_both(place, weight, src_ref, acc_ref):
    def step(b, sums):
        other = [src_ref[k, pl.ds(b, 1), :] for k in range(4)]
        offset = [place[k] - other[k] for k in range(3)]
        square = offset[0] * offset[0] + offset[1] * offset[1] + (offset[2] * offset[2] + SOFTENING)
        inverse = lax.rsqrt(square)
        margin = jnp.maximum(DIAMETER - square * inverse, 0.0)
        push = margin * inverse * (weight + other[3])
        terms = [push * d for d in offset] + [margin]
        for k in range(4):
            acc_ref[k, pl.ds(pl.multiple_of(b * 8, 8), 8), :] = jnp.sum(terms[k].reshape(HALF // 8, 8, LANES), axis=0)
        return tuple(total + term for total, term in zip(sums, terms))

    zero = jnp.zeros((HALF, LANES), F32)
    return lax.fori_loop(0, MEMBERS, step, (zero, zero, zero, zero), unroll=4)


def source_sums(acc_ref):
    out = []
    for k in range(4):
        rows = [acc_ref[k, pl.ds(r, MEMBERS, stride=8), :] for r in range(8)]
        out.append(((rows[0] + rows[1]) + (rows[2] + rows[3])) + ((rows[4] + rows[5]) + (rows[6] + rows[7])))
    return out


def place_of(brick):
    return jnp.bitwise_xor(brick, FIRST)


def in_order(rows):
    blocks = [rows[8 * k : 8 * k + 8] for k in range(BRICKS // 4)]
    return jnp.concatenate([blocks[(FIRST // 4) ^ k] for k in range(BRICKS // 4)], 0)


def routes(leaving, dest):
    to = one_hot(dest, BRICKS)
    before = lax.broadcasted_iota(I32, (PAIRS, PAIRS), 0) < lax.broadcasted_iota(I32, (PAIRS, PAIRS), 1)
    before = jnp.where(before, 1.0, 0.0).astype(BF16)
    earlier = jnp.dot(to, before, preferred_element_type=F32)
    rank = jnp.sum(earlier * to.astype(F32), axis=0, keepdims=True).astype(I32)
    column = one_hot(place_of(dest) * SLOT_CAP + rank, BRICKS * SLOT_CAP)
    leaves = one_hot(leaving)
    ones = jnp.ones((8, PAIRS), F32).astype(BF16)
    return (
        lax.dot_general(column, leaves, LAST, preferred_element_type=F32),
        lax.dot_general(ones, leaves, LAST, preferred_element_type=F32),
    )


def pack_kernel(
    pos_hbm,
    ori_hbm,
    hist_hbm,
    velocity_hbm,
    template_hbm,
    local_hbm,
    ghost_hbm,
    first_hbm,
    gap_hbm,
    leaving_hbm,
    dest_hbm,
    count_ref,
    packed_ref,
    velocity_ref,
    template_ref,
    local_ref,
    ghost_ref,
    first_ref,
    gap_ref,
    leaving_ref,
    dest_ref,
    pos_ref,
    ori_ref,
    sems,
):
    moves = [
        (hist_hbm, packed_ref.at[0:MEMBERS]),
        (pos_hbm, pos_ref),
        (ori_hbm, ori_ref),
        (local_hbm, local_ref),
        (ghost_hbm, ghost_ref),
        (leaving_hbm, leaving_ref),
        (dest_hbm, dest_ref),
        (velocity_hbm, velocity_ref),
        (template_hbm, template_ref),
        (first_hbm, first_ref),
        (gap_hbm, gap_ref),
    ]
    copies = [pltpu.make_async_copy(a, b, sems.at[k]) for k, (a, b) in enumerate(moves)]
    for copy in copies:
        copy.start()
    for copy in copies[1:]:
        copy.wait()
    live = lax.broadcasted_iota(I32, (1, PAIRS), 1) < count_ref[0]
    ghost = ghost_ref[...]
    code = jnp.where(live, ghost, ghost + IDLE)
    lists = jnp.concatenate([local_ref[...], local_ref[...], code, code], 1).astype(F32)
    packed_ref[MEMBERS:PACKED] = jnp.concatenate([pos_ref[...], ori_ref[...], lists], 0)
    copies[0].wait()


def inner_kernel(
    packed_ref,
    template_ref,
    first_ref,
    gap_ref,
    leaving_ref,
    dest_ref,
    totals_ref,
    route_ref,
    departed_ref,
    spread_ref,
    src_ref,
    acc_ref,
):
    template = spread_template(template_ref)
    for k in range(3):
        spread_ref[k] = template[k]
    route_ref[...], departed_ref[...] = routes(leaving_ref[...], dest_ref[...])

    own = parts_of(packed_ref[...])
    first = first_ref[...]
    second = one_hot(twice(jnp.bitwise_and(first + gap_ref[...], CLUMPS - 1)))
    first = one_hot(twice(first))
    picked = gather(own, second)
    arm_b = arms_of(picked, template)
    place_source(src_ref, picked, arm_b, (0.0, 0.0, 0.0))
    place, weight, arm = half_targets(gather(own, first), template)
    rows = half_rows(arm, contact_both(place, weight, src_ref, acc_ref))
    force_x, force_y, force_z, margin = source_sums(acc_ref)
    other = jnp.concatenate([margin, -body_rows(arm_b, (force_x, force_y, force_z))], 0)
    totals_ref[...] = scatter(rows, first) + scatter(other, second)


def outer_kernel(
    packed_ref,
    totals_ref,
    velocity_ref,
    spread_ref,
    local_ref,
    ghost_ref,
    count_ref,
    route_ref,
    slab_next_ref,
    brick_next_ref,
    brick_back_ref,
    slab_back_ref,
    state_ref,
    buffer_ref,
    src_ref,
    src2_ref,
):
    template = [spread_ref[k] for k in range(3)]
    lane = lax.broadcasted_iota(I32, (1, LANES), 1)
    low = lane < PAIRS
    live = lax.broadcasted_iota(I32, (1, PAIRS), 1) < count_ref[0]
    local_code = twice(jnp.where(live, local_ref[...], IDLE))
    local = twice(local_ref[...])
    ghost = twice(ghost_ref[...])
    brick_lists = brick_back_ref[LISTS : LISTS + 1].astype(I32)
    slab_lists = slab_back_ref[LISTS : LISTS + 1].astype(I32)
    brick_local, brick_code = brick_lists[:, :LANES], brick_lists[:, LANES:]
    slab_local, slab_code = slab_lists[:, :LANES], slab_lists[:, LANES:]

    own = parts_of(packed_ref[...])
    source = (
        gather(parts_of(brick_next_ref[...]), one_hot(jnp.where(low, ghost, -1)))
        + gather(parts_of(slab_next_ref[...]), one_hot(jnp.where(low, ghost - CLUMPS, -1)))
        + gather(parts_of(brick_back_ref[...]), one_hot(jnp.where(low, -1, brick_local)))
    )
    near = ghost < CLUMPS
    shift = (
        jnp.where(low, jnp.where(near, 0.0, 1.0), 0.0),
        jnp.where(low, jnp.where(near, 1.0, 0.0), -1.0),
        0.0,
    )
    place_source(src_ref, source, arms_of(source, template), shift)
    picked = gather(own, one_hot(jnp.where(low, local, jnp.bitwise_and(brick_code, CLUMPS - 1))))
    source = gather(parts_of(slab_back_ref[...]), one_hot(slab_local))
    place_source(src2_ref, source, arms_of(source, template), (-1.0, 0.0, 0.0))
    chosen = one_hot(jnp.bitwise_and(slab_code, CLUMPS - 1))
    place, weight, arm = half_targets(gather(own, chosen), template)

    rows2 = half_rows(arm, contact(place, weight, src2_ref))
    rows = full_batch(picked, template, src_ref)
    totals = (
        totals_ref[...]
        + scatter(rows2, one_hot(slab_code - CLUMPS))
        + scatter(rows, one_hot(jnp.where(low, local_code, brick_code)))
    )

    state = packed_ref[...]
    velocity = velocity_ref[...]
    ow, ox, oy, oz = orient = [state[ORI + k : ORI + k + 1] for k in range(4)]
    linear = velocity[0:3] + TIME_STEP * totals[MEMBERS : MEMBERS + 3]
    angular = velocity[3:6] + TIME_STEP * totals[MEMBERS + 3 : MEMBERS + 6] / INERTIA_SCALE
    centre = state[POS : POS + 3] + TIME_STEP * linear
    wx, wy, wz = [angular[k : k + 1] for k in range(3)]
    spin = [
        -(wx * ox + wy * oy + wz * oz),
        ow * wx + (wy * oz - wz * oy),
        ow * wy + (wz * ox - wx * oz),
        ow * wz + (wx * oy - wy * ox),
    ]
    turned = [orient[k] + 0.5 * TIME_STEP * spin[k] for k in range(4)]
    history = HISTORY_DECAY * state[0:MEMBERS] + totals[0:MEMBERS]
    full = jnp.concatenate(
        [history, centre] + turned + [linear, angular, jnp.zeros((LANES - 77, CLUMPS), F32)], 0
    )
    state_ref[...] = full
    slots = lax.dot_general(route_ref[...].astype(BF16), parts_of(full), LAST, preferred_element_type=F32)
    buffer_ref[...] = slots[:, :LANES] + slots[:, LANES : 2 * LANES] + slots[:, 2 * LANES :]


def stay_kernel(state_ref, departed_ref, staying_ref):
    departed = departed_ref[0:1] > 0.5
    staying_ref[0:13] = jnp.where(departed, 0.0, state_ref[MEMBERS : MEMBERS + 13])
    staying_ref[13:77] = jnp.where(departed, 0.0, state_ref[0:MEMBERS])


def turn_kernel(in_ref, out_ref):
    turned = in_order(in_ref[...]).T
    out_ref[0:13] = turned[MEMBERS : MEMBERS + 13]
    out_ref[13:77] = turned[0:MEMBERS]


def vmem():
    return pl.BlockSpec(memory_space=pltpu.VMEM)


def smem():
    return pl.BlockSpec(memory_space=pltpu.SMEM)


def hbm():
    return pl.BlockSpec(memory_space=pltpu.HBM)


def small():
    return pltpu.CompilerParams(vmem_limit_bytes=VMEM_LIMIT)


def cost(flops):
    return pl.CostEstimate(flops=flops, bytes_accessed=400_000, transcendentals=flops // 30)


def array(*shape, dtype=F32):
    return jax.ShapeDtypeStruct(shape, dtype)


def from_behind(value, axis, steps):
    count = lax.axis_size(axis)
    pairs = [(source, (source + steps) % count) for source in range(count)]
    return lax.ppermute(value, axis, pairs)


def shards(
    position,
    orient,
    velocity,
    history,
    template,
    cross_local,
    cross_ghost,
    cross_count,
    inner_first,
    inner_gap,
    mig_index,
    mig_dest,
):
    lists = [v.reshape(1, PAIRS) for v in (cross_local, cross_ghost, inner_first, inner_gap, mig_index, mig_dest)]
    loads = [
        pltpu.with_memory_space_constraint(v, pltpu.HBM)
        for v in (position, orient, history, velocity, template, *lists)
    ]
    packed, velocity, template, local, ghost, first, gap, leaving, dest = pl.pallas_call(
        pack_kernel,
        out_shape=(array(PACKED, CLUMPS), array(6, CLUMPS), array(3, MEMBERS)) + (array(1, PAIRS, dtype=I32),) * 6,
        in_specs=[hbm()] * 11 + [smem()],
        out_specs=(vmem(),) * 9,
        scratch_shapes=[
            pltpu.VMEM((3, CLUMPS), F32),
            pltpu.VMEM((4, CLUMPS), F32),
            pltpu.SemaphoreType.DMA((11,)),
        ],
        compiler_params=small(),
        name="pack",
    )(*loads, cross_count)
    slab_next = from_behind(packed, "slab", -1)
    slab_back = from_behind(packed, "slab", 1)
    brick_next = from_behind(packed, "brick", -1)
    brick_back = from_behind(packed, "brick", 1)
    totals, route, departed, spread = pl.pallas_call(
        inner_kernel,
        out_shape=(
            array(PACKED, CLUMPS),
            array(BRICKS * SLOT_CAP, CLUMPS),
            array(8, CLUMPS),
            array(3, MEMBERS, LANES),
        ),
        in_specs=[vmem()] * 6,
        out_specs=(vmem(),) * 4,
        scratch_shapes=[
            pltpu.VMEM((4, MEMBERS, LANES), F32),
            pltpu.VMEM((4, 8 * MEMBERS, LANES), F32),
        ],
        cost_estimate=cost(20_000_000),
        compiler_params=small(),
        name="inner",
    )(packed, template, first, gap, leaving, dest)
    state, buffer = pl.pallas_call(
        outer_kernel,
        out_shape=(array(LANES, CLUMPS), array(BRICKS * SLOT_CAP, LANES)),
        in_specs=[vmem()] * 6 + [smem()] + [vmem()] * 5,
        out_specs=(vmem(),) * 2,
        scratch_shapes=[pltpu.VMEM((4, MEMBERS, LANES), F32)] * 2,
        cost_estimate=cost(25_000_000),
        compiler_params=small(),
        name="outer",
    )(
        packed,
        totals,
        velocity,
        spread,
        local,
        ghost,
        cross_count,
        route,
        slab_next,
        brick_next,
        brick_back,
        slab_back,
    )
    arrived = lax.all_to_all(
        buffer.reshape(BRICKS, SLOT_CAP, LANES),
        "brick",
        split_axis=0,
        concat_axis=0,
        axis_index_groups=[ORDER],
    )
    staying = pl.pallas_call(
        stay_kernel,
        out_shape=array(77, CLUMPS),
        in_specs=[vmem()] * 2,
        out_specs=vmem(),
        cost_estimate=cost(5_000_000),
        compiler_params=small(),
        name="stay",
    )(state, departed)
    arrivals = pl.pallas_call(
        turn_kernel,
        out_shape=array(77, BRICKS * SLOT_CAP),
        in_specs=[vmem()],
        out_specs=vmem(),
        compiler_params=small(),
        name="turn",
    )(arrived.reshape(BRICKS * SLOT_CAP, LANES))
    return (staying, arrivals)


def solution(mesh):
    both = ("slab", "brick")
    return jax.shard_map(
        shards,
        mesh=mesh,
        in_specs=(
            P(None, both),
            P(None, both),
            P(None, both),
            P(None, both),
            P(),
            P(both),
            P(both),
            P(both),
            P(both),
            P(both),
            P(both),
            P(both, None),
        ),
        out_specs=(P(None, both), P(None, both)),
        check_vma=False,
    )
```

time: 45.1 us -> 43.9 us (0.973)
  the two profiles are of different devices: /device:TPU:6 before, /device:TPU:1 now
where the time goes in v4:
time: 43.9 us; the launch traced here: 43.7 us
  starting transfers between devices  30.2 us (69%)
  Pallas kernels  8.72 us (20%)
  waiting for transfers between devices  3.35 us (8%)
  between operations  1.35 us (3%)
    ppermute x4, starting transfers between devices, from_behind(): return lax.ppermute(value, axis, pairs)  18.1 us
    all_to_all x1, starting transfers between devices, shards(): lax.all_to_all(buffer.reshape(BRICKS, SLOT_CAP, LANES), 'brick', split_ax...  12.1 us
    pallas_call x1, Pallas kernels, shards(): pl.pallas_call(outer_kernel, out_shape=(array(LANES, CLUMPS), array(BRICK...  4.5 us
    ppermute x4, waiting for transfers between devices, from_behind(): return lax.ppermute(value, axis, pairs)  1.88 us
    pallas_call x1, Pallas kernels, shards(): pl.pallas_call(inner_kernel, out_shape=(array(PACKED, CLUMPS), array(BRIC...  1.85 us
    all_to_all x1, waiting for transfers between devices, shards(): lax.all_to_all(buffer.reshape(BRICKS, SLOT_CAP, LANES), 'brick', split_ax...  1.47 us
    pallas_call x1, Pallas kernels, shards(): pl.pallas_call(pack_kernel, out_shape=(array(PACKED, CLUMPS), array(6, CL...  1.01 us
  transfers between devices with their start and end apart: 5, of which 2 were waited for; matrix products, arithmetic and copies ran while one was open for 0% of the time, Pallas kernels for 6%

profile of v4, /device:TPU:1, one launch (start us, length us, event | category | flops | bytes accessed | tf_op | source)
XLA Modules:
  0.0 43.7 jit_solution(2942759341469203449)
XLA Ops:
  1.3 1.0 %pack.1 = (f32[72,256]{1,0:T(8,128)S(1)}, f32[6,256]{1,0:T(8,128)S(1)}, f32[3,64]{1,0:T(4,128)S(1)}, s32[1,64]{1,0:T(1,128)S(1)}, s32[1,64]{1,0:T(1,128)S(1)}, /...) custom-call(f32[3,256]{1,0:T(4,128)} %pos_hbm.1, f32[4,256]{1,0:T(4,128)} %ori_hbm.1, ...), custom_call_target="tpu_custom_call" | custom-call | tf_op jit(solution)/shard_map/pack/pallas_call | solution.py:427
  2.3 2.6 %collective-permute-start.3 = (f32[72,256]{1,0:T(8,128)S(1)}, f32[72,256]{1,0:T(8,128)S(1)}, u32[]{:S(2)}, u32[]{:S(2)}) collective-permute-start(f32[72,256]{1,0:T(8,128)S(1)} %get-tuple-element.17.packed_ref), channel_id=1, source_target_pairs={{0,64},{64,128},{128,192},{192,256},{256,320},{320,384},{384,448},... | collective-permute-start | bytes 221192 | tf_op jit(solution)/shard_map/ppermute | solution.py:405
  4.9 4.0 %collective-permute-start.2 = (f32[72,256]{1,0:T(8,128)S(1)}, f32[72,256]{1,0:T(8,128)S(1)}, u32[]{:S(2)}, u32[]{:S(2)}) collective-permute-start(f32[72,256]{1,0:T(8,128)S(1)} %get-tuple-element.17.packed_ref), channel_id=1, source_target_pairs={{0,1},{1,2},{2,3},{3,4},{4,5},{5,6},{6,7},{7,8},{8,9},{9,10},{10,1... | collective-permute-start | bytes 221192 | tf_op jit(solution)/shard_map/ppermute | solution.py:405
  8.9 11.5 %collective-permute-start.1 = (f32[72,256]{1,0:T(8,128)S(1)}, f32[72,256]{1,0:T(8,128)S(1)}, u32[]{:S(2)}, u32[]{:S(2)}) collective-permute-start(f32[72,256]{1,0:T(8,128)S(1)} %get-tuple-element.17.packed_ref), channel_id=1, source_target_pairs={{0,63},{1,0},{2,1},{3,2},{4,3},{5,4},{6,5},{7,6},{8,7},{9,8},{10,9... | collective-permute-start | bytes 221192 | tf_op jit(solution)/shard_map/ppermute | solution.py:405
  20.4 0.0 collective-permute-start
  20.4 1.9 %inner.1 = (f32[72,256]{1,0:T(8,128)S(1)}, f32[128,256]{1,0:T(8,128)S(1)}, f32[8,256]{1,0:T(8,128)S(1)}, f32[3,64,128]{2,1,0:T(8,128)S(1)}) custom-call(f32[72,256]{1,0:T(8,128)S(1)} %get-tuple-element.17.packed_ref, f32[3,64]{1,0:T(4,128)S(1)} %get-tuple-element.18.template_ref, s32[1,64]{1,0:T(1,128)S(1)} %get-tuple-element.19.first_ref, ...), custom_call_target="tpu_custom_call" | custom-call | flops 20000000 | bytes 400000 | tf_op jit(solution)/shard_map/inner/pallas_call | solution.py:444
  22.3 0.0 collective-permute-done.3.slab_back_ref
  22.3 0.0 collective-permute-done.2.brick_back_ref
  22.3 0.0 collective-permute-done.1.brick_next_ref
  22.3 1.9 %collective-permute-done.slab_next_ref = f32[72,256]{1,0:T(8,128)S(1)} collective-permute-done((f32[72,256]{1,0:T(8,128)S(1)}, f32[72,256]{1,0:T(8,128)S(1)}, u32[]{:S(2)}, u32[]{:S(2)}) %collective-permute-start) | collective-permute-done | bytes 73760 | tf_op jit(solution)/shard_map/ppermute | solution.py:405
  24.2 4.5 %outer.1 = (f32[128,256]{1,0:T(8,128)S(1)}, f32[128,128]{1,0:T(8,128)}) custom-call(f32[72,256]{1,0:T(8,128)S(1)} %get-tuple-element.17.packed_ref, f32[72,256]{1,0:T(8,128)S(1)} %get-tuple-element.23.totals_ref, f32[6,256]{1,0:T(8,128)S(1)} %get-tuple-element.24.velocity_ref, f32[3,64,128]{2,1,0:T(8,128)S(1)} %get-tuple-element.25.spread_ref, ...), custom_call_target="tpu_custom_call" | custom-call | flops 25000000 | bytes 400000 | tf_op jit(solution)/shard_map/outer/pallas_call | solution.py:462
  28.7 12.1 %all-to-all-start = ((f32[64,2,128]{2,1,0:T(2,128)}), f32[64,2,128]{2,1,0:T(2,128)S(1)}, u32[]{:S(2)}, u32[]{:S(2)}) async-start(f32[64,2,128]{2,1,0:T(2,128)} %bitcast.6), calls=%async_computation | async-start | bytes 131072 | tf_op jit(solution)/shard_map/all_to_all | solution.py:485
  40.8 0.6 %stay.1 = f32[77,256]{1,0:T(8,128)} custom-call(f32[128,256]{1,0:T(8,128)S(1)} %get-tuple-element.29.state_ref, f32[8,256]{1,0:T(8,128)S(1)} %get-tuple-element.30.departed_ref), custom_call_target="tpu_custom_call" | custom-call | flops 5000000 | bytes 400000 | tf_op jit(solution)/shard_map/stay/pallas_call | solution.py:492
  41.5 1.5 %all-to-all-done = f32[64,2,128]{2,1,0:T(2,128)S(1)} async-done(((f32[64,2,128]{2,1,0:T(2,128)}), f32[64,2,128]{2,1,0:T(2,128)S(1)}, u32[]{:S(2)}, u32[]{:S(2)}) %all-to-all-start) | async-done | bytes 65568 | tf_op jit(solution)/shard_map/all_to_all | solution.py:485
  43.0 0.7 %turn.1 = f32[77,128]{1,0:T(8,128)} custom-call(f32[128,128]{1,0:T(8,128)S(1)} %bitcast.8), custom_call_target="tpu_custom_call" | custom-call | tf_op jit(solution)/shard_map/turn/pallas_call | solution.py:501
Async XLA Ops:
  2.3 20.0 %collective-permute-start.3 = (f32[72,256]{1,0:T(8,128)S(1)}, f32[72,256]{1,0:T(8,128)S(1)}, u32[]{:S(2)}, u32[]{:S(2)}) collective-permute-start(f32[72,256]{1,0:T(8,128)S(1)} %get-tuple-element.17.packed_ref), channel_id=1, source_target_pairs={{0,64},{64,128},{128,192},{192,256},{256,320},{320,384},{384,448},... | collective-permute-start | bytes 221192 | tf_op jit(solution)/shard_map/ppermute | solution.py:405
  4.9 17.4 %collective-permute-start.2 = (f32[72,256]{1,0:T(8,128)S(1)}, f32[72,256]{1,0:T(8,128)S(1)}, u32[]{:S(2)}, u32[]{:S(2)}) collective-permute-start(f32[72,256]{1,0:T(8,128)S(1)} %get-tuple-element.17.packed_ref), channel_id=1, source_target_pairs={{0,1},{1,2},{2,3},{3,4},{4,5},{5,6},{6,7},{7,8},{8,9},{9,10},{10,1... | collective-permute-start | bytes 221192 | tf_op jit(solution)/shard_map/ppermute | solution.py:405
  8.9 13.4 %collective-permute-start.1 = (f32[72,256]{1,0:T(8,128)S(1)}, f32[72,256]{1,0:T(8,128)S(1)}, u32[]{:S(2)}, u32[]{:S(2)}) collective-permute-start(f32[72,256]{1,0:T(8,128)S(1)} %get-tuple-element.17.packed_ref), channel_id=1, source_target_pairs={{0,63},{1,0},{2,1},{3,2},{4,3},{5,4},{6,5},{7,6},{8,7},{9,8},{10,9... | collective-permute-start | bytes 221192 | tf_op jit(solution)/shard_map/ppermute | solution.py:405
  20.4 3.8 %collective-permute-start = (f32[72,256]{1,0:T(8,128)S(1)}, f32[72,256]{1,0:T(8,128)S(1)}, u32[]{:S(2)}, u32[]{:S(2)}) collective-permute-start(f32[72,256]{1,0:T(8,128)S(1)} %get-tuple-element.17.packed_ref), channel_id=1, source_target_pairs={{0,448},{64,0},{128,64},{192,128},{256,192},{320,256},{384,320},{4... | collective-permute-start | bytes 221192 | tf_op jit(solution)/shard_map/ppermute | solution.py:405
  28.7 14.3 %all-to-all-start = ((f32[64,2,128]{2,1,0:T(2,128)}), f32[64,2,128]{2,1,0:T(2,128)S(1)}, u32[]{:S(2)}, u32[]{:S(2)}) async-start(f32[64,2,128]{2,1,0:T(2,128)} %bitcast.6), calls=%async_computation | async-start | bytes 131072 | tf_op jit(solution)/shard_map/all_to_all | solution.py:485

commit v5 on v4

--- a/solution.py
+++ b/solution.py
@@ -12,7 +12,7 @@
 HALF = MEMBERS // 2
 SLOT_CAP = 2
 BRICKS = 64
-FIRST = 36
+FIRST = 52
 ORDER = [FIRST ^ k for k in range(BRICKS)]
 VMEM_LIMIT = 8 * 1024 * 1024
 IDLE = 1024
@@ -257,10 +257,12 @@
     gap_ref,
     leaving_ref,
     dest_ref,
+    local_ref,
     totals_ref,
     route_ref,
     departed_ref,
     spread_ref,
+    target_ref,
     src_ref,
     acc_ref,
 ):
@@ -270,6 +272,12 @@
     route_ref[...], departed_ref[...] = routes(leaving_ref[...], dest_ref[...])
 
     own = parts_of(packed_ref[...])
+    place, weight, arm = half_targets(gather(own, one_hot(twice(local_ref[...]))), template)
+    for k in range(3):
+        target_ref[k] = place[k]
+        target_ref[4 + k] = arm[k]
+    target_ref[3] = weight
+
     first = first_ref[...]
     second = one_hot(twice(jnp.bitwise_and(first + gap_ref[...], CLUMPS - 1)))
     first = one_hot(twice(first))
@@ -283,62 +291,52 @@
     totals_ref[...] = scatter(rows, first) + scatter(other, second)
 
 
+def before_kernel(packed_ref, inner_ref, spread_ref, brick_back_ref, slab_back_ref, totals_ref, src_ref):
+    template = [spread_ref[k] for k in range(3)]
+    low = lax.broadcasted_iota(I32, (1, LANES), 1) < PAIRS
+    brick_lists = brick_back_ref[LISTS : LISTS + 1].astype(I32)
+    slab_lists = slab_back_ref[LISTS : LISTS + 1].astype(I32)
+    brick_local, brick_code = brick_lists[:, :LANES], brick_lists[:, LANES:]
+    slab_local, slab_code = slab_lists[:, :LANES], slab_lists[:, LANES:]
+    source = gather(parts_of(brick_back_ref[...]), one_hot(jnp.where(low, brick_local, -1))) + gather(
+        parts_of(slab_back_ref[...]), one_hot(jnp.where(low, -1, slab_local))
+    )
+    shift = (jnp.where(low, 0.0, -1.0), jnp.where(low, -1.0, 0.0), 0.0)
+    place_source(src_ref, source, arms_of(source, template), shift)
+    chosen = one_hot(jnp.bitwise_and(jnp.where(low, brick_code, slab_code), CLUMPS - 1))
+    rows = full_batch(gather(parts_of(packed_ref[...]), chosen), template, src_ref)
+    totals_ref[...] = inner_ref[...] + scatter(rows, one_hot(jnp.where(low, brick_code, slab_code - CLUMPS)))
+
+
 def outer_kernel(
     packed_ref,
     totals_ref,
     velocity_ref,
     spread_ref,
+    target_ref,
     local_ref,
     ghost_ref,
     count_ref,
     route_ref,
+    brick_next_ref,
     slab_next_ref,
-    brick_next_ref,
-    brick_back_ref,
-    slab_back_ref,
     state_ref,
     buffer_ref,
     src_ref,
-    src2_ref,
 ):
     template = [spread_ref[k] for k in range(3)]
-    lane = lax.broadcasted_iota(I32, (1, LANES), 1)
-    low = lane < PAIRS
     live = lax.broadcasted_iota(I32, (1, PAIRS), 1) < count_ref[0]
-    local_code = twice(jnp.where(live, local_ref[...], IDLE))
-    local = twice(local_ref[...])
+    local = twice(jnp.where(live, local_ref[...], IDLE))
     ghost = twice(ghost_ref[...])
-    brick_lists = brick_back_ref[LISTS : LISTS + 1].astype(I32)
-    slab_lists = slab_back_ref[LISTS : LISTS + 1].astype(I32)
-    brick_local, brick_code = brick_lists[:, :LANES], brick_lists[:, LANES:]
-    slab_local, slab_code = slab_lists[:, :LANES], slab_lists[:, LANES:]
-
-    own = parts_of(packed_ref[...])
-    source = (
-        gather(parts_of(brick_next_ref[...]), one_hot(jnp.where(low, ghost, -1)))
-        + gather(parts_of(slab_next_ref[...]), one_hot(jnp.where(low, ghost - CLUMPS, -1)))
-        + gather(parts_of(brick_back_ref[...]), one_hot(jnp.where(low, -1, brick_local)))
-    )
     near = ghost < CLUMPS
-    shift = (
-        jnp.where(low, jnp.where(near, 0.0, 1.0), 0.0),
-        jnp.where(low, jnp.where(near, 1.0, 0.0), -1.0),
-        0.0,
-    )
+    source = gather(parts_of(brick_next_ref[...]), one_hot(ghost)) + gather(
+        parts_of(slab_next_ref[...]), one_hot(ghost - CLUMPS)
+    )
+    shift = (jnp.where(near, 0.0, 1.0), jnp.where(near, 1.0, 0.0), 0.0)
     place_source(src_ref, source, arms_of(source, template), shift)
-    picked = gather(own, one_hot(jnp.where(low, local, jnp.bitwise_and(brick_code, CLUMPS - 1))))
-    source = gather(parts_of(slab_back_ref[...]), one_hot(slab_local))
-    place_source(src2_ref, source, arms_of(source, template), (-1.0, 0.0, 0.0))
-    chosen = one_hot(jnp.bitwise_and(slab_code, CLUMPS - 1))
-    place, weight, arm = half_targets(gather(own, chosen), template)
-
-    rows2 = half_rows(arm, contact(place, weight, src2_ref))
-    rows = full_batch(picked, template, src_ref)
-    totals = (
-        totals_ref[...]
-        + scatter(rows2, one_hot(slab_code - CLUMPS))
-        + scatter(rows, one_hot(jnp.where(low, local_code, brick_code)))
-    )
+    out = contact([target_ref[k] for k in range(3)], target_ref[3], src_ref)
+    rows = half_rows([target_ref[4 + k] for k in range(3)], out)
+    totals = totals_ref[...] + scatter(rows, one_hot(local))
 
     state = packed_ref[...]
     velocity = velocity_ref[...]
@@ -363,16 +361,13 @@
     buffer_ref[...] = slots[:, :LANES] + slots[:, LANES : 2 * LANES] + slots[:, 2 * LANES :]
 
 
-def stay_kernel(state_ref, departed_ref, staying_ref):
+def finish_kernel(arrived_ref, state_ref, departed_ref, staying_ref, arrivals_ref):
     departed = departed_ref[0:1] > 0.5
     staying_ref[0:13] = jnp.where(departed, 0.0, state_ref[MEMBERS : MEMBERS + 13])
     staying_ref[13:77] = jnp.where(departed, 0.0, state_ref[0:MEMBERS])
-
-
-def turn_kernel(in_ref, out_ref):
-    turned = in_order(in_ref[...]).T
-    out_ref[0:13] = turned[MEMBERS : MEMBERS + 13]
-    out_ref[13:77] = turned[0:MEMBERS]
+    turned = in_order(arrived_ref[...]).T
+    arrivals_ref[0:13] = turned[MEMBERS : MEMBERS + 13]
+    arrivals_ref[13:77] = turned[0:MEMBERS]
 
 
 def vmem():
@@ -441,16 +436,17 @@
     slab_back = from_behind(packed, "slab", 1)
     brick_next = from_behind(packed, "brick", -1)
     brick_back = from_behind(packed, "brick", 1)
-    totals, route, departed, spread = pl.pallas_call(
+    totals, route, departed, spread, target = pl.pallas_call(
         inner_kernel,
         out_shape=(
             array(PACKED, CLUMPS),
             array(BRICKS * SLOT_CAP, CLUMPS),
             array(8, CLUMPS),
             array(3, MEMBERS, LANES),
+            array(7, HALF, LANES),
         ),
-        in_specs=[vmem()] * 6,
-        out_specs=(vmem(),) * 4,
+        in_specs=[vmem()] * 7,
+        out_specs=(vmem(),) * 5,
         scratch_shapes=[
             pltpu.VMEM((4, MEMBERS, LANES), F32),
             pltpu.VMEM((4, 8 * MEMBERS, LANES), F32),
@@ -458,14 +454,24 @@
         cost_estimate=cost(20_000_000),
         compiler_params=small(),
         name="inner",
-    )(packed, template, first, gap, leaving, dest)
+    )(packed, template, first, gap, leaving, dest, local)
+    totals = pl.pallas_call(
+        before_kernel,
+        out_shape=array(PACKED, CLUMPS),
+        in_specs=[vmem()] * 5,
+        out_specs=vmem(),
+        scratch_shapes=[pltpu.VMEM((4, MEMBERS, LANES), F32)],
+        cost_estimate=cost(20_000_000),
+        compiler_params=small(),
+        name="before",
+    )(packed, totals, spread, brick_back, slab_back)
     state, buffer = pl.pallas_call(
         outer_kernel,
         out_shape=(array(LANES, CLUMPS), array(BRICKS * SLOT_CAP, LANES)),
-        in_specs=[vmem()] * 6 + [smem()] + [vmem()] * 5,
+        in_specs=[vmem()] * 7 + [smem()] + [vmem()] * 3,
         out_specs=(vmem(),) * 2,
-        scratch_shapes=[pltpu.VMEM((4, MEMBERS, LANES), F32)] * 2,
-        cost_estimate=cost(25_000_000),
+        scratch_shapes=[pltpu.VMEM((4, MEMBERS, LANES), F32)],
+        cost_estimate=cost(15_000_000),
         compiler_params=small(),
         name="outer",
     )(
@@ -473,14 +479,13 @@
         totals,
         velocity,
         spread,
+        target,
         local,
         ghost,
         cross_count,
         route,
+        brick_next,
         slab_next,
-        brick_next,
-        brick_back,
-        slab_back,
     )
     arrived = lax.all_to_all(
         buffer.reshape(BRICKS, SLOT_CAP, LANES),
@@ -489,23 +494,15 @@
         concat_axis=0,
         axis_index_groups=[ORDER],
     )
-    staying = pl.pallas_call(
-        stay_kernel,
-        out_shape=array(77, CLUMPS),
-        in_specs=[vmem()] * 2,
-        out_specs=vmem(),
+    staying, arrivals = pl.pallas_call(
+        finish_kernel,
+        out_shape=(array(77, CLUMPS), array(77, BRICKS * SLOT_CAP)),
+        in_specs=[vmem()] * 3,
+        out_specs=(vmem(),) * 2,
         cost_estimate=cost(5_000_000),
         compiler_params=small(),
-        name="stay",
-    )(state, departed)
-    arrivals = pl.pallas_call(
-        turn_kernel,
-        out_shape=array(77, BRICKS * SLOT_CAP),
-        in_specs=[vmem()],
-        out_specs=vmem(),
-        compiler_params=small(),
-        name="turn",
-    )(arrived.reshape(BRICKS * SLOT_CAP, LANES))
+        name="finish",
+    )(arrived.reshape(BRICKS * SLOT_CAP, LANES), state, departed)
     return (staying, arrivals)
 
 

time: 43.9 us -> 42.2 us (0.961)
  the two profiles are of different devices: /device:TPU:1 before, /device:TPU:6 now
where the time goes in v5:
time: 42.2 us; the launch traced here: 41.5 us
  starting transfers between devices  17.2 us (41%)
  blocking collectives  15.1 us (36%)
  Pallas kernels  7.78 us (18%)
  between operations  1.37 us (3%)
    ppermute x4, starting transfers between devices, from_behind(): return lax.ppermute(value, axis, pairs)  17.2 us
    all_to_all x1, blocking collectives, shards(): lax.all_to_all(buffer.reshape(BRICKS, SLOT_CAP, LANES), 'brick', split_ax...  15.1 us
    pallas_call x1, Pallas kernels, shards(): pl.pallas_call(before_kernel, out_shape=array(PACKED, CLUMPS), in_specs=[...  2.42 us
    pallas_call x1, Pallas kernels, shards(): pl.pallas_call(inner_kernel, out_shape=(array(PACKED, CLUMPS), array(BRIC...  1.93 us
    pallas_call x1, Pallas kernels, shards(): pl.pallas_call(outer_kernel, out_shape=(array(LANES, CLUMPS), array(BRICK...  1.72 us
    pallas_call x1, Pallas kernels, shards(): pl.pallas_call(pack_kernel, out_shape=(array(PACKED, CLUMPS), array(6, CL...  1.01 us
  transfers between devices with their start and end apart: 4, of which 0 were waited for; matrix products, arithmetic and copies ran while one was open for 0% of the time, Pallas kernels for 10%

profile of v5, /device:TPU:6, one launch (start us, length us, event | category | flops | bytes accessed | tf_op | source)
XLA Modules:
  0.0 41.5 jit_solution(13501956666636567809)
XLA Ops:
  1.3 1.0 %pack.1 = (f32[72,256]{1,0:T(8,128)S(1)}, f32[6,256]{1,0:T(8,128)S(1)}, f32[3,64]{1,0:T(4,128)S(1)}, s32[1,64]{1,0:T(1,128)S(1)}, s32[1,64]{1,0:T(1,128)S(1)}, /...) custom-call(f32[3,256]{1,0:T(4,128)} %pos_hbm.1, f32[4,256]{1,0:T(4,128)} %ori_hbm.1, ...), custom_call_target="tpu_custom_call" | custom-call | tf_op jit(solution)/shard_map/pack/pallas_call | solution.py:422
  2.3 4.3 %collective-permute-start = (f32[72,256]{1,0:T(8,128)S(1)}, f32[72,256]{1,0:T(8,128)S(1)}, u32[]{:S(2)}, u32[]{:S(2)}) collective-permute-start(f32[72,256]{1,0:T(8,128)S(1)} %get-tuple-element.18.packed_ref), channel_id=1, source_target_pairs={{0,1},{1,2},{2,3},{3,4},{4,5},{5,6},{6,7},{7,8},{8,9},{9,10},{10,1... | collective-permute-start | bytes 221192 | tf_op jit(solution)/shard_map/ppermute | solution.py:400
  6.6 0.0 collective-permute-start.1
  6.6 11.5 %collective-permute-start.2 = (f32[72,256]{1,0:T(8,128)S(1)}, f32[72,256]{1,0:T(8,128)S(1)}, u32[]{:S(2)}, u32[]{:S(2)}) collective-permute-start(f32[72,256]{1,0:T(8,128)S(1)} %get-tuple-element.18.packed_ref), channel_id=1, source_target_pairs={{0,63},{1,0},{2,1},{3,2},{4,3},{5,4},{6,5},{7,6},{8,7},{9,8},{10,9... | collective-permute-start | bytes 221192 | tf_op jit(solution)/shard_map/ppermute | solution.py:400
  18.1 1.5 %collective-permute-start.3 = (f32[72,256]{1,0:T(8,128)S(1)}, f32[72,256]{1,0:T(8,128)S(1)}, u32[]{:S(2)}, u32[]{:S(2)}) collective-permute-start(f32[72,256]{1,0:T(8,128)S(1)} %get-tuple-element.18.packed_ref), channel_id=1, source_target_pairs={{0,448},{64,0},{128,64},{192,128},{256,192},{320,256},{384,320},{4... | collective-permute-start | bytes 221192 | tf_op jit(solution)/shard_map/ppermute | solution.py:400
  19.6 1.9 %inner.1 = (f32[72,256]{1,0:T(8,128)S(1)}, f32[128,256]{1,0:T(8,128)S(1)}, f32[8,256]{1,0:T(8,128)S(1)}, f32[3,64,128]{2,1,0:T(8,128)S(1)}, f32[7,32,128]{2,1,0:T(8,128)S(1)}) custom-call(f32[72,256]{1,0:T(8,128)S(1)} %get-tuple-element.18.packed_ref, f32[3,64]{1,0:T(4,128)S(1)} %get-tuple-element.19.template_ref, s32[1,64]{1,0:T(1,128)S(1)} %get-tuple-element.20.first_ref, ...), custom_call_target="tpu_custom_call" | custom-call | flops 20000000 | bytes 400000 | tf_op jit(solution)/shard_map/inner/pallas_call | solution.py:439
  21.5 0.0 collective-permute-done.brick_back_ref
  21.5 0.0 collective-permute-done.1.slab_back_ref
  21.5 2.4 %before.1.totals_ref = f32[72,256]{1,0:T(8,128)S(1)} custom-call(f32[72,256]{1,0:T(8,128)S(1)} %get-tuple-element.18.packed_ref, f32[72,256]{1,0:T(8,128)S(1)} %get-tuple-element.25.inner_ref, f32[3,64,128]{2,1,0:T(8,128)S(1)} %get-tuple-element.26.spread_ref, f32[72,256]{1,0:T(8,128)S(1)} %collective-permute-done.brick_back_ref, ...), custom_call_target="tpu_custom_call" | custom-call | flops 20000000 | bytes 400000 | tf_op jit(solution)/shard_map/before/pallas_call | solution.py:458
  23.9 0.0 collective-permute-done.2.brick_next_ref
  24.0 0.0 collective-permute-done.3.slab_next_ref
  24.0 1.7 %outer.1 = (f32[128,256]{1,0:T(8,128)S(1)}, f32[128,128]{1,0:T(8,128)S(1)}) custom-call(f32[72,256]{1,0:T(8,128)S(1)} %get-tuple-element.18.packed_ref, f32[72,256]{1,0:T(8,128)S(1)} %before.1.totals_ref, f32[6,256]{1,0:T(8,128)S(1)} %get-tuple-element.27.velocity_ref, f32[3,64,128]{2,1,0:T(8,128)S(1)} %get-tuple-element.26.spread_ref, ...), custom_call_target="tpu_custom_call" | custom-call | flops 15000000 | bytes 400000 | tf_op jit(solution)/shard_map/outer/pallas_call | solution.py:468
  25.7 15.1 %all_to_all.5 = f32[64,2,128]{2,1,0:T(2,128)S(1)} all-to-all(f32[64,2,128]{2,1,0:T(2,128)S(1)} %bitcast.8), channel_id=1, replica_groups={{52,53,54,55,48,49,50,51,60,61,62,63,56,57,58,59,36,37,38,39,32,33,34,3..., dimensions={0} | all-to-all | bytes 131072 | tf_op jit(solution)/shard_map/all_to_all | solution.py:490
  40.8 0.7 %finish.1 = (f32[77,256]{1,0:T(8,128)}, f32[77,128]{1,0:T(8,128)}) custom-call(f32[128,128]{1,0:T(8,128)S(1)} %bitcast.9, f32[128,256]{1,0:T(8,128)S(1)} %get-tuple-element.32.state_ref, f32[8,256]{1,0:T(8,128)S(1)} %get-tuple-element.33.departed_ref), custom_call_target="tpu_custom_call" | custom-call | flops 5000000 | bytes 400000 | tf_op jit(solution)/shard_map/finish/pallas_call | solution.py:497
Async XLA Ops:
  2.3 19.2 %collective-permute-start = (f32[72,256]{1,0:T(8,128)S(1)}, f32[72,256]{1,0:T(8,128)S(1)}, u32[]{:S(2)}, u32[]{:S(2)}) collective-permute-start(f32[72,256]{1,0:T(8,128)S(1)} %get-tuple-element.18.packed_ref), channel_id=1, source_target_pairs={{0,1},{1,2},{2,3},{3,4},{4,5},{5,6},{6,7},{7,8},{8,9},{9,10},{10,1... | collective-permute-start | bytes 221192 | tf_op jit(solution)/shard_map/ppermute | solution.py:400
  6.6 14.9 %collective-permute-start.1 = (f32[72,256]{1,0:T(8,128)S(1)}, f32[72,256]{1,0:T(8,128)S(1)}, u32[]{:S(2)}, u32[]{:S(2)}) collective-permute-start(f32[72,256]{1,0:T(8,128)S(1)} %get-tuple-element.18.packed_ref), channel_id=1, source_target_pairs={{0,64},{64,128},{128,192},{192,256},{256,320},{320,384},{384,448},... | collective-permute-start | bytes 221192 | tf_op jit(solution)/shard_map/ppermute | solution.py:400
  6.6 17.3 %collective-permute-start.2 = (f32[72,256]{1,0:T(8,128)S(1)}, f32[72,256]{1,0:T(8,128)S(1)}, u32[]{:S(2)}, u32[]{:S(2)}) collective-permute-start(f32[72,256]{1,0:T(8,128)S(1)} %get-tuple-element.18.packed_ref), channel_id=1, source_target_pairs={{0,63},{1,0},{2,1},{3,2},{4,3},{5,4},{6,5},{7,6},{8,7},{9,8},{10,9... | collective-permute-start | bytes 221192 | tf_op jit(solution)/shard_map/ppermute | solution.py:400
  18.1 5.8 %collective-permute-start.3 = (f32[72,256]{1,0:T(8,128)S(1)}, f32[72,256]{1,0:T(8,128)S(1)}, u32[]{:S(2)}, u32[]{:S(2)}) collective-permute-start(f32[72,256]{1,0:T(8,128)S(1)} %get-tuple-element.18.packed_ref), channel_id=1, source_target_pairs={{0,448},{64,0},{128,64},{192,128},{256,192},{320,256},{384,320},{4... | collective-permute-start | bytes 221192 | tf_op jit(solution)/shard_map/ppermute | solution.py:400

commit v6 on v5

--- a/solution.py
+++ b/solution.py
@@ -105,7 +105,7 @@
         return (sums[0] + push * dx, sums[1] + push * dy, sums[2] + push * dz, sums[3] + margin)
 
     zero = jnp.zeros((HALF, LANES), F32)
-    return lax.fori_loop(0, MEMBERS, step, (zero, zero, zero, zero), unroll=4)
+    return lax.fori_loop(0, MEMBERS, step, (zero, zero, zero, zero), unroll=16)
 
 
 def body_rows(arm, force):
@@ -163,7 +163,7 @@
         return tuple(total + term for total, term in zip(sums, terms))
 
     zero = jnp.zeros((HALF, LANES), F32)
-    return lax.fori_loop(0, MEMBERS, step, (zero, zero, zero, zero), unroll=4)
+    return lax.fori_loop(0, MEMBERS, step, (zero, zero, zero, zero), unroll=16)
 
 
 def source_sums(acc_ref):
@@ -293,19 +293,48 @@
 
 def before_kernel(packed_ref, inner_ref, spread_ref, brick_back_ref, slab_back_ref, totals_ref, src_ref):
     template = [spread_ref[k] for k in range(3)]
-    low = lax.broadcasted_iota(I32, (1, LANES), 1) < PAIRS
+    lane = lax.broadcasted_iota(I32, (1, LANES), 1)
+    low = lane < PAIRS
     brick_lists = brick_back_ref[LISTS : LISTS + 1].astype(I32)
     slab_lists = slab_back_ref[LISTS : LISTS + 1].astype(I32)
-    brick_local, brick_code = brick_lists[:, :LANES], brick_lists[:, LANES:]
-    slab_local, slab_code = slab_lists[:, :LANES], slab_lists[:, LANES:]
-    source = gather(parts_of(brick_back_ref[...]), one_hot(jnp.where(low, brick_local, -1))) + gather(
-        parts_of(slab_back_ref[...]), one_hot(jnp.where(low, -1, slab_local))
-    )
-    shift = (jnp.where(low, 0.0, -1.0), jnp.where(low, -1.0, 0.0), 0.0)
-    place_source(src_ref, source, arms_of(source, template), shift)
-    chosen = one_hot(jnp.bitwise_and(jnp.where(low, brick_code, slab_code), CLUMPS - 1))
-    rows = full_batch(gather(parts_of(packed_ref[...]), chosen), template, src_ref)
-    totals_ref[...] = inner_ref[...] + scatter(rows, one_hot(jnp.where(low, brick_code, slab_code - CLUMPS)))
+    local = jnp.where(low, brick_lists[:, :LANES], slab_lists[:, :LANES])
+    code = jnp.where(low, brick_lists[:, LANES:], slab_lists[:, LANES:] - CLUMPS)
+    live = (code >= 0) & (code < CLUMPS)
+    before = lax.broadcasted_iota(I32, (LANES, LANES), 0) < lax.broadcasted_iota(I32, (LANES, LANES), 1)
+    before = jnp.where(before, 1.0, 0.0).astype(BF16)
+    flags = jnp.broadcast_to(jnp.where(live, 1.0, 0.0), (16, LANES)).astype(BF16)
+    place = jnp.dot(flags, before, preferred_element_type=F32)[0:1].astype(I32)
+    place = jnp.where(live, place, -1)
+    count = jnp.max(place) + 1
+    source = gather(parts_of(brick_back_ref[...]), one_hot(jnp.where(low, local, -1))) + gather(
+        parts_of(slab_back_ref[...]), one_hot(jnp.where(low, -1, local))
+    )
+    target = gather(parts_of(packed_ref[...]), one_hot(jnp.bitwise_and(code, CLUMPS - 1)))
+    ones = jnp.ones((1, LANES), F32)
+    side = jnp.where(low, 1.0, 0.0)
+    both = jnp.concatenate(
+        [source[:LISTS], ones, target[:LISTS], code.astype(F32), side, jnp.zeros((7, LANES), F32)], 0
+    )
+    both = parts_of(both)
+    totals_ref[...] = inner_ref[...]
+
+    def batch(k, carry):
+        slot = jnp.bitwise_and(lax.broadcasted_iota(I32, (LANES, LANES), 0), PAIRS - 1) + k * PAIRS
+        chosen = jnp.where(slot == place, 1.0, 0.0).astype(F32).astype(BF16)
+        taken = sum_parts(lax.dot_general(both, chosen, LAST, preferred_element_type=F32))
+        source, target, side = taken[:PACKED], taken[PACKED : 2 * PACKED], taken[2 * PACKED : 2 * PACKED + 1]
+        filled = source[LISTS : LISTS + 1]
+        fill = jnp.where(lax.broadcasted_iota(I32, (PACKED, LANES), 0) == ORI, 1.0 - filled, 0.0)
+        source = source + fill
+        clump = jnp.where(filled > 0.5, target[LISTS:PACKED], float(IDLE)).astype(I32)
+        target = target + fill
+        place_source(src_ref, source, arms_of(source, template), (side - 1.0, -side, 0.0))
+        spot, weight, arm = half_targets(target, template)
+        rows = half_rows(arm, contact(spot, weight, src_ref))
+        totals_ref[...] += scatter(rows, one_hot(clump))
+        return carry
+
+    lax.fori_loop(0, jnp.where(count > PAIRS, 2, 1), batch, 0)
 
 
 def outer_kernel(

time: 42.2 us -> 41.4 us (0.981)
  Pallas kernels: 7.78 us -> 6.91 us
    pallas_call x1, Pallas kernels: 2.42 us -> 1.74 us  [shards(): pl.pallas_call(before_kernel, out_shape=array(PACKED, CLUMPS), in_specs=[...]
  transfers between devices with their start and end apart: 4 -> 4, of which waited for: 0 -> 0; matrix products, arithmetic and copies ran while one was open for 0% -> 0% of each run, Pallas kernels for 10% -> 9%
where the time goes in v6:
time: 41.4 us; the launch traced here: 40.7 us
  starting transfers between devices  17.2 us (42%)
  blocking collectives  15.1 us (36%)
  Pallas kernels  6.91 us (17%)
  between operations  1.37 us (3%)
    ppermute x4, starting transfers between devices, from_behind(): return lax.ppermute(value, axis, pairs)  17.2 us
    all_to_all x1, blocking collectives, shards(): lax.all_to_all(buffer.reshape(BRICKS, SLOT_CAP, LANES), 'brick', split_ax...  15.1 us
    pallas_call x1, Pallas kernels, shards(): pl.pallas_call(inner_kernel, out_shape=(array(PACKED, CLUMPS), array(BRIC...  1.81 us
    pallas_call x1, Pallas kernels, shards(): pl.pallas_call(before_kernel, out_shape=array(PACKED, CLUMPS), in_specs=[...  1.74 us
    pallas_call x1, Pallas kernels, shards(): pl.pallas_call(outer_kernel, out_shape=(array(LANES, CLUMPS), array(BRICK...  1.64 us
    pallas_call x1, Pallas kernels, shards(): pl.pallas_call(pack_kernel, out_shape=(array(PACKED, CLUMPS), array(6, CL...  1.01 us
  transfers between devices with their start and end apart: 4, of which 0 were waited for; matrix products, arithmetic and copies ran while one was open for 0% of the time, Pallas kernels for 9%

profile of v6, /device:TPU:6, one launch (start us, length us, event | category | flops | bytes accessed | tf_op | source)
XLA Modules:
  0.0 40.7 jit_solution(7190600850511954014)
XLA Ops:
  1.3 1.0 %pack.1 = (f32[72,256]{1,0:T(8,128)S(1)}, f32[6,256]{1,0:T(8,128)S(1)}, f32[3,64]{1,0:T(4,128)S(1)}, s32[1,64]{1,0:T(1,128)S(1)}, s32[1,64]{1,0:T(1,128)S(1)}, /...) custom-call(f32[3,256]{1,0:T(4,128)} %pos_hbm.1, f32[4,256]{1,0:T(4,128)} %ori_hbm.1, ...), custom_call_target="tpu_custom_call" | custom-call | tf_op jit(solution)/shard_map/pack/pallas_call | solution.py:451
  2.3 4.3 %collective-permute-start = (f32[72,256]{1,0:T(8,128)S(1)}, f32[72,256]{1,0:T(8,128)S(1)}, u32[]{:S(2)}, u32[]{:S(2)}) collective-permute-start(f32[72,256]{1,0:T(8,128)S(1)} %get-tuple-element.18.packed_ref), channel_id=1, source_target_pairs={{0,1},{1,2},{2,3},{3,4},{4,5},{5,6},{6,7},{7,8},{8,9},{9,10},{10,1... | collective-permute-start | bytes 221192 | tf_op jit(solution)/shard_map/ppermute | solution.py:429
  6.6 0.0 collective-permute-start.1
  6.6 11.5 %collective-permute-start.2 = (f32[72,256]{1,0:T(8,128)S(1)}, f32[72,256]{1,0:T(8,128)S(1)}, u32[]{:S(2)}, u32[]{:S(2)}) collective-permute-start(f32[72,256]{1,0:T(8,128)S(1)} %get-tuple-element.18.packed_ref), channel_id=1, source_target_pairs={{0,63},{1,0},{2,1},{3,2},{4,3},{5,4},{6,5},{7,6},{8,7},{9,8},{10,9... | collective-permute-start | bytes 221192 | tf_op jit(solution)/shard_map/ppermute | solution.py:429
  18.1 1.5 %collective-permute-start.3 = (f32[72,256]{1,0:T(8,128)S(1)}, f32[72,256]{1,0:T(8,128)S(1)}, u32[]{:S(2)}, u32[]{:S(2)}) collective-permute-start(f32[72,256]{1,0:T(8,128)S(1)} %get-tuple-element.18.packed_ref), channel_id=1, source_target_pairs={{0,448},{64,0},{128,64},{192,128},{256,192},{320,256},{384,320},{4... | collective-permute-start | bytes 221192 | tf_op jit(solution)/shard_map/ppermute | solution.py:429
  19.6 1.8 %inner.1 = (f32[72,256]{1,0:T(8,128)S(1)}, f32[128,256]{1,0:T(8,128)S(1)}, f32[8,256]{1,0:T(8,128)S(1)}, f32[3,64,128]{2,1,0:T(8,128)S(1)}, f32[7,32,128]{2,1,0:T(8,128)S(1)}) custom-call(f32[72,256]{1,0:T(8,128)S(1)} %get-tuple-element.18.packed_ref, f32[3,64]{1,0:T(4,128)S(1)} %get-tuple-element.19.template_ref, s32[1,64]{1,0:T(1,128)S(1)} %get-tuple-element.20.first_ref, ...), custom_call_target="tpu_custom_call" | custom-call | flops 20000000 | bytes 400000 | tf_op jit(solution)/shard_map/inner/pallas_call | solution.py:468
  21.4 0.0 collective-permute-done.brick_back_ref
  21.4 0.0 collective-permute-done.1.slab_back_ref
  21.4 1.7 %before.1.totals_ref = f32[72,256]{1,0:T(8,128)S(1)} custom-call(f32[72,256]{1,0:T(8,128)S(1)} %get-tuple-element.18.packed_ref, f32[72,256]{1,0:T(8,128)S(1)} %get-tuple-element.25.inner_ref, f32[3,64,128]{2,1,0:T(8,128)S(1)} %get-tuple-element.26.spread_ref, f32[72,256]{1,0:T(8,128)S(1)} %collective-permute-done.brick_back_ref, ...), custom_call_target="tpu_custom_call" | custom-call | flops 20000000 | bytes 400000 | tf_op jit(solution)/shard_map/before/pallas_call | solution.py:487
  23.1 0.0 collective-permute-done.2.brick_next_ref
  23.2 0.0 collective-permute-done.3.slab_next_ref
  23.2 1.6 %outer.1 = (f32[128,256]{1,0:T(8,128)S(1)}, f32[128,128]{1,0:T(8,128)S(1)}) custom-call(f32[72,256]{1,0:T(8,128)S(1)} %get-tuple-element.18.packed_ref, f32[72,256]{1,0:T(8,128)S(1)} %before.1.totals_ref, f32[6,256]{1,0:T(8,128)S(1)} %get-tuple-element.27.velocity_ref, f32[3,64,128]{2,1,0:T(8,128)S(1)} %get-tuple-element.26.spread_ref, ...), custom_call_target="tpu_custom_call" | custom-call | flops 15000000 | bytes 400000 | tf_op jit(solution)/shard_map/outer/pallas_call | solution.py:497
  24.8 15.1 %all_to_all.5 = f32[64,2,128]{2,1,0:T(2,128)S(1)} all-to-all(f32[64,2,128]{2,1,0:T(2,128)S(1)} %bitcast.8), channel_id=1, replica_groups={{52,53,54,55,48,49,50,51,60,61,62,63,56,57,58,59,36,37,38,39,32,33,34,3..., dimensions={0} | all-to-all | bytes 131072 | tf_op jit(solution)/shard_map/all_to_all | solution.py:519
  40.0 0.7 %finish.1 = (f32[77,256]{1,0:T(8,128)}, f32[77,128]{1,0:T(8,128)}) custom-call(f32[128,128]{1,0:T(8,128)S(1)} %bitcast.9, f32[128,256]{1,0:T(8,128)S(1)} %get-tuple-element.32.state_ref, f32[8,256]{1,0:T(8,128)S(1)} %get-tuple-element.33.departed_ref), custom_call_target="tpu_custom_call" | custom-call | flops 5000000 | bytes 400000 | tf_op jit(solution)/shard_map/finish/pallas_call | solution.py:526
Async XLA Ops:
  2.3 19.1 %collective-permute-start = (f32[72,256]{1,0:T(8,128)S(1)}, f32[72,256]{1,0:T(8,128)S(1)}, u32[]{:S(2)}, u32[]{:S(2)}) collective-permute-start(f32[72,256]{1,0:T(8,128)S(1)} %get-tuple-element.18.packed_ref), channel_id=1, source_target_pairs={{0,1},{1,2},{2,3},{3,4},{4,5},{5,6},{6,7},{7,8},{8,9},{9,10},{10,1... | collective-permute-start | bytes 221192 | tf_op jit(solution)/shard_map/ppermute | solution.py:429
  6.6 14.8 %collective-permute-start.1 = (f32[72,256]{1,0:T(8,128)S(1)}, f32[72,256]{1,0:T(8,128)S(1)}, u32[]{:S(2)}, u32[]{:S(2)}) collective-permute-start(f32[72,256]{1,0:T(8,128)S(1)} %get-tuple-element.18.packed_ref), channel_id=1, source_target_pairs={{0,64},{64,128},{128,192},{192,256},{256,320},{320,384},{384,448},... | collective-permute-start | bytes 221192 | tf_op jit(solution)/shard_map/ppermute | solution.py:429
  6.6 16.5 %collective-permute-start.2 = (f32[72,256]{1,0:T(8,128)S(1)}, f32[72,256]{1,0:T(8,128)S(1)}, u32[]{:S(2)}, u32[]{:S(2)}) collective-permute-start(f32[72,256]{1,0:T(8,128)S(1)} %get-tuple-element.18.packed_ref), channel_id=1, source_target_pairs={{0,63},{1,0},{2,1},{3,2},{4,3},{5,4},{6,5},{7,6},{8,7},{9,8},{10,9... | collective-permute-start | bytes 221192 | tf_op jit(solution)/shard_map/ppermute | solution.py:429
  18.1 5.0 %collective-permute-start.3 = (f32[72,256]{1,0:T(8,128)S(1)}, f32[72,256]{1,0:T(8,128)S(1)}, u32[]{:S(2)}, u32[]{:S(2)}) collective-permute-start(f32[72,256]{1,0:T(8,128)S(1)} %get-tuple-element.18.packed_ref), channel_id=1, source_target_pairs={{0,448},{64,0},{128,64},{192,128},{256,192},{320,256},{384,320},{4... | collective-permute-start | bytes 221192 | tf_op jit(solution)/shard_map/ppermute | solution.py:429

commit v7 on v6

--- a/solution.py
+++ b/solution.py
@@ -105,7 +105,7 @@
         return (sums[0] + push * dx, sums[1] + push * dy, sums[2] + push * dz, sums[3] + margin)
 
     zero = jnp.zeros((HALF, LANES), F32)
-    return lax.fori_loop(0, MEMBERS, step, (zero, zero, zero, zero), unroll=16)
+    return lax.fori_loop(0, MEMBERS, step, (zero, zero, zero, zero), unroll=32)
 
 
 def body_rows(arm, force):
@@ -163,7 +163,7 @@
         return tuple(total + term for total, term in zip(sums, terms))
 
     zero = jnp.zeros((HALF, LANES), F32)
-    return lax.fori_loop(0, MEMBERS, step, (zero, zero, zero, zero), unroll=16)
+    return lax.fori_loop(0, MEMBERS, step, (zero, zero, zero, zero), unroll=32)
 
 
 def source_sums(acc_ref):

time: 41.4 us -> 41.3 us (level)
  no operation moved by 1% of the time
where the time goes in v7:
time: 41.3 us; the launch traced here: 40.6 us
  starting transfers between devices  17.2 us (42%)
  blocking collectives  15.1 us (37%)
  Pallas kernels  6.82 us (17%)
  between operations  1.37 us (3%)
    ppermute x4, starting transfers between devices, from_behind(): return lax.ppermute(value, axis, pairs)  17.2 us
    all_to_all x1, blocking collectives, shards(): lax.all_to_all(buffer.reshape(BRICKS, SLOT_CAP, LANES), 'brick', split_ax...  15.1 us
    pallas_call x1, Pallas kernels, shards(): pl.pallas_call(inner_kernel, out_shape=(array(PACKED, CLUMPS), array(BRIC...  1.78 us
    pallas_call x1, Pallas kernels, shards(): pl.pallas_call(before_kernel, out_shape=array(PACKED, CLUMPS), in_specs=[...  1.71 us
    pallas_call x1, Pallas kernels, shards(): pl.pallas_call(outer_kernel, out_shape=(array(LANES, CLUMPS), array(BRICK...  1.61 us
    pallas_call x1, Pallas kernels, shards(): pl.pallas_call(pack_kernel, out_shape=(array(PACKED, CLUMPS), array(6, CL...  1.01 us
  transfers between devices with their start and end apart: 4, of which 0 were waited for; matrix products, arithmetic and copies ran while one was open for 0% of the time, Pallas kernels for 9%

profile of v7, /device:TPU:6, one launch (start us, length us, event | category | flops | bytes accessed | tf_op | source)
XLA Modules:
  0.0 40.6 jit_solution(4605950562993091939)
XLA Ops:
  1.3 1.0 %pack.1 = (f32[72,256]{1,0:T(8,128)S(1)}, f32[6,256]{1,0:T(8,128)S(1)}, f32[3,64]{1,0:T(4,128)S(1)}, s32[1,64]{1,0:T(1,128)S(1)}, s32[1,64]{1,0:T(1,128)S(1)}, /...) custom-call(f32[3,256]{1,0:T(4,128)} %pos_hbm.1, f32[4,256]{1,0:T(4,128)} %ori_hbm.1, ...), custom_call_target="tpu_custom_call" | custom-call | tf_op jit(solution)/shard_map/pack/pallas_call | solution.py:451
  2.3 4.3 %collective-permute-start = (f32[72,256]{1,0:T(8,128)S(1)}, f32[72,256]{1,0:T(8,128)S(1)}, u32[]{:S(2)}, u32[]{:S(2)}) collective-permute-start(f32[72,256]{1,0:T(8,128)S(1)} %get-tuple-element.18.packed_ref), channel_id=1, source_target_pairs={{0,1},{1,2},{2,3},{3,4},{4,5},{5,6},{6,7},{7,8},{8,9},{9,10},{10,1... | collective-permute-start | bytes 221192 | tf_op jit(solution)/shard_map/ppermute | solution.py:429
  6.6 0.0 collective-permute-start.1
  6.6 11.5 %collective-permute-start.2 = (f32[72,256]{1,0:T(8,128)S(1)}, f32[72,256]{1,0:T(8,128)S(1)}, u32[]{:S(2)}, u32[]{:S(2)}) collective-permute-start(f32[72,256]{1,0:T(8,128)S(1)} %get-tuple-element.18.packed_ref), channel_id=1, source_target_pairs={{0,63},{1,0},{2,1},{3,2},{4,3},{5,4},{6,5},{7,6},{8,7},{9,8},{10,9... | collective-permute-start | bytes 221192 | tf_op jit(solution)/shard_map/ppermute | solution.py:429
  18.1 1.5 %collective-permute-start.3 = (f32[72,256]{1,0:T(8,128)S(1)}, f32[72,256]{1,0:T(8,128)S(1)}, u32[]{:S(2)}, u32[]{:S(2)}) collective-permute-start(f32[72,256]{1,0:T(8,128)S(1)} %get-tuple-element.18.packed_ref), channel_id=1, source_target_pairs={{0,448},{64,0},{128,64},{192,128},{256,192},{320,256},{384,320},{4... | collective-permute-start | bytes 221192 | tf_op jit(solution)/shard_map/ppermute | solution.py:429
  19.6 1.8 %inner.1 = (f32[72,256]{1,0:T(8,128)S(1)}, f32[128,256]{1,0:T(8,128)S(1)}, f32[8,256]{1,0:T(8,128)S(1)}, f32[3,64,128]{2,1,0:T(8,128)S(1)}, f32[7,32,128]{2,1,0:T(8,128)S(1)}) custom-call(f32[72,256]{1,0:T(8,128)S(1)} %get-tuple-element.18.packed_ref, f32[3,64]{1,0:T(4,128)S(1)} %get-tuple-element.19.template_ref, s32[1,64]{1,0:T(1,128)S(1)} %get-tuple-element.20.first_ref, ...), custom_call_target="tpu_custom_call" | custom-call | flops 20000000 | bytes 400000 | tf_op jit(solution)/shard_map/inner/pallas_call | solution.py:468
  21.4 0.0 collective-permute-done.brick_back_ref
  21.4 0.0 collective-permute-done.1.slab_back_ref
  21.4 1.7 %before.1.totals_ref = f32[72,256]{1,0:T(8,128)S(1)} custom-call(f32[72,256]{1,0:T(8,128)S(1)} %get-tuple-element.18.packed_ref, f32[72,256]{1,0:T(8,128)S(1)} %get-tuple-element.25.inner_ref, f32[3,64,128]{2,1,0:T(8,128)S(1)} %get-tuple-element.26.spread_ref, f32[72,256]{1,0:T(8,128)S(1)} %collective-permute-done.brick_back_ref, ...), custom_call_target="tpu_custom_call" | custom-call | flops 20000000 | bytes 400000 | tf_op jit(solution)/shard_map/before/pallas_call | solution.py:487
  23.1 0.0 collective-permute-done.2.brick_next_ref
  23.1 0.0 collective-permute-done.3.slab_next_ref
  23.1 1.6 %outer.1 = (f32[128,256]{1,0:T(8,128)S(1)}, f32[128,128]{1,0:T(8,128)S(1)}) custom-call(f32[72,256]{1,0:T(8,128)S(1)} %get-tuple-element.18.packed_ref, f32[72,256]{1,0:T(8,128)S(1)} %before.1.totals_ref, f32[6,256]{1,0:T(8,128)S(1)} %get-tuple-element.27.velocity_ref, f32[3,64,128]{2,1,0:T(8,128)S(1)} %get-tuple-element.26.spread_ref, ...), custom_call_target="tpu_custom_call" | custom-call | flops 15000000 | bytes 400000 | tf_op jit(solution)/shard_map/outer/pallas_call | solution.py:497
  24.7 15.1 %all_to_all.5 = f32[64,2,128]{2,1,0:T(2,128)S(1)} all-to-all(f32[64,2,128]{2,1,0:T(2,128)S(1)} %bitcast.8), channel_id=1, replica_groups={{52,53,54,55,48,49,50,51,60,61,62,63,56,57,58,59,36,37,38,39,32,33,34,3..., dimensions={0} | all-to-all | bytes 131072 | tf_op jit(solution)/shard_map/all_to_all | solution.py:519
  39.9 0.7 %finish.1 = (f32[77,256]{1,0:T(8,128)}, f32[77,128]{1,0:T(8,128)}) custom-call(f32[128,128]{1,0:T(8,128)S(1)} %bitcast.9, f32[128,256]{1,0:T(8,128)S(1)} %get-tuple-element.32.state_ref, f32[8,256]{1,0:T(8,128)S(1)} %get-tuple-element.33.departed_ref), custom_call_target="tpu_custom_call" | custom-call | flops 5000000 | bytes 400000 | tf_op jit(solution)/shard_map/finish/pallas_call | solution.py:526
Async XLA Ops:
  2.3 19.1 %collective-permute-start = (f32[72,256]{1,0:T(8,128)S(1)}, f32[72,256]{1,0:T(8,128)S(1)}, u32[]{:S(2)}, u32[]{:S(2)}) collective-permute-start(f32[72,256]{1,0:T(8,128)S(1)} %get-tuple-element.18.packed_ref), channel_id=1, source_target_pairs={{0,1},{1,2},{2,3},{3,4},{4,5},{5,6},{6,7},{7,8},{8,9},{9,10},{10,1... | collective-permute-start | bytes 221192 | tf_op jit(solution)/shard_map/ppermute | solution.py:429
  6.6 14.8 %collective-permute-start.1 = (f32[72,256]{1,0:T(8,128)S(1)}, f32[72,256]{1,0:T(8,128)S(1)}, u32[]{:S(2)}, u32[]{:S(2)}) collective-permute-start(f32[72,256]{1,0:T(8,128)S(1)} %get-tuple-element.18.packed_ref), channel_id=1, source_target_pairs={{0,64},{64,128},{128,192},{192,256},{256,320},{320,384},{384,448},... | collective-permute-start | bytes 221192 | tf_op jit(solution)/shard_map/ppermute | solution.py:429
  6.6 16.5 %collective-permute-start.2 = (f32[72,256]{1,0:T(8,128)S(1)}, f32[72,256]{1,0:T(8,128)S(1)}, u32[]{:S(2)}, u32[]{:S(2)}) collective-permute-start(f32[72,256]{1,0:T(8,128)S(1)} %get-tuple-element.18.packed_ref), channel_id=1, source_target_pairs={{0,63},{1,0},{2,1},{3,2},{4,3},{5,4},{6,5},{7,6},{8,7},{9,8},{10,9... | collective-permute-start | bytes 221192 | tf_op jit(solution)/shard_map/ppermute | solution.py:429
  18.1 5.0 %collective-permute-start.3 = (f32[72,256]{1,0:T(8,128)S(1)}, f32[72,256]{1,0:T(8,128)S(1)}, u32[]{:S(2)}, u32[]{:S(2)}) collective-permute-start(f32[72,256]{1,0:T(8,128)S(1)} %get-tuple-element.18.packed_ref), channel_id=1, source_target_pairs={{0,448},{64,0},{128,64},{192,128},{256,192},{320,256},{384,320},{4... | collective-permute-start | bytes 221192 | tf_op jit(solution)/shard_map/ppermute | solution.py:429
